TPU v7x, 128 devices: a whole 4x4x4 slice. The times are simulated.
128 devices in a mesh: dp: 16 (over x, z), mp: 8 (over y, core).
Axes of the slice: x: 4, y: 4, z: 4, core: 2. Of those that a mesh axis runs over, the one named last changes fastest.
Arguments:
- enc: bfloat16 [2048, 4096], P('dp'), may hold values from -6 to 6
- dec: bfloat16 [4096, 4096], P('dp'), may hold values from -6 to 6
- grad_out: bfloat16 [4096, 4096], P('dp'), may hold values from -6 to 6
- w_query: bfloat16 [4096, 4096], P(None, 'mp'), may hold values from -0.09375 to 0.09375
- w_key: bfloat16 [4096, 4096], P(None, 'mp'), may hold values from -0.09375 to 0.09375
- w_value: bfloat16 [4096, 4096], P(None, 'mp'), may hold values from -0.09375 to 0.09375
- w_out: bfloat16 [4096, 4096], P('mp'), may hold values from -0.09375 to 0.09375
- enc_len: int32 [16, 16], replicated, may hold values from 1 to 16, 128 in all within a row
- dec_len: int32 [16, 16], replicated, may hold values from 1 to 32, 256 in all within a row
- device_perm: int32 [16], replicated, may hold values from 0 to 15, each once
- slot_offset: int32 [16], replicated, may hold values from 0 to 15, each once
Outputs:
- mixed: bfloat16 [4096, 4096], P('dp')
- dec_grad: bfloat16 [4096, 4096], P('dp')
- enc_grad: bfloat16 [2048, 4096], P('dp')
- grad_query: float32 [4096, 4096], P('dp', 'mp')
- grad_key: float32 [4096, 4096], P('dp', 'mp')
- grad_value: float32 [4096, 4096], P('dp', 'mp')
- grad_proj: float32 [4096, 4096], P('mp', 'dp')
Inputs may be any that keep to these rules, and one draw needn't show every extreme that they name: enc_len[i] are the input lengths of the examples packed in order on device i's encoder rows; one of them is 16 on every device. dec_len[j] are the target lengths of the examples packed in order on device j's decoder rows.
All inputs are finite; a program needn't handle non-finite values.
Results may differ from a plain program's by a relative error of at most 0.023.
Values may be sent and summed in bfloat16 or wider, within the bound.
A program may use at most 192 MiB of HBM per device.

v0:
```python
import jax
import jax.numpy as jnp
from jax import lax
from jax.sharding import PartitionSpec as P

DK = 256


EPS = 1e-06
LOGIT_DIVISOR = 10.0


def contract_rows(former, latter):
    return lax.dot_general(
        former, latter, (((0,), (0,)), ((), ())), preferred_element_type=jnp.float32
    )


def contract_cols(former, latter):
    return lax.dot_general(
        former, latter, (((1,), (1,)), ((), ())), preferred_element_type=jnp.float32
    )


def normalize(inputs):
    factor = lax.rsqrt(jnp.mean(inputs * inputs, axis=-1, keepdims=True) + EPS)
    return (inputs * factor, factor)


def norm_back(upstream, unit_rows, factor):
    return factor * (upstream - unit_rows * jnp.mean(upstream * unit_rows, axis=-1, keepdims=True))


def slot_table(example_lengths, row_count):
    run_ends = jnp.cumsum(example_lengths, axis=1, dtype=jnp.int32)
    positions = jnp.arange(row_count, dtype=jnp.int32)
    return jnp.sum(
        (positions[None, :, None] >= run_ends[:, None, :]).astype(jnp.int32),
        axis=2,
        dtype=jnp.int32,
    )


def owner_table(device_perm, slot_offset, ex_count):
    devices = device_perm.shape[0]
    wrapped = (
        jnp.arange(devices, dtype=jnp.int32)[:, None] + slot_offset[None, :ex_count]
    ) % devices
    return jnp.take(device_perm, wrapped, axis=0)


def lookup(per_slot, slot_ids):
    ex_count = per_slot.shape[1]
    onehot = (slot_ids[:, :, None] == jnp.arange(ex_count, dtype=jnp.int32)[None, None, :]).astype(
        jnp.int32
    )
    return jnp.sum(onehot * per_slot[:, None, :], axis=2, dtype=jnp.int32)


def attend(asking_projection_table, key_rows, value_rows, upstream, allowed):
    logit_divisor_amount = LOGIT_DIVISOR / asking_projection_table.shape[-1]
    pairwise_logits = (
        jnp.einsum(
            "aic,oic->iao", asking_projection_table, key_rows, preferred_element_type=jnp.float32
        )
        * logit_divisor_amount
    )
    weights = jnp.where(allowed[None], jnp.exp(pairwise_logits), 0.0).astype(jnp.bfloat16)
    totals = jnp.sum(weights.astype(jnp.float32), axis=2)
    mixed_heads = (
        jnp.einsum("hqk,khd->qhd", weights, value_rows, preferred_element_type=jnp.float32)
        / jnp.transpose(totals)[:, :, None]
    )
    attention_weighting = weights.astype(jnp.float32) / totals[:, :, None]
    weighting_cotangent = jnp.einsum(
        "aic,oic->iao", upstream, value_rows, preferred_element_type=jnp.float32
    )
    weighted_inner_correction = jnp.transpose(
        jnp.sum(upstream.astype(jnp.float32) * mixed_heads, axis=2)
    )
    logit_cotangent = (
        attention_weighting
        * (weighting_cotangent - weighted_inner_correction[:, :, None])
        * logit_divisor_amount
    ).astype(jnp.bfloat16)
    dquery = jnp.einsum(
        "hqk,khd->qhd", logit_cotangent, key_rows, preferred_element_type=jnp.float32
    )
    grad_keys = jnp.einsum(
        "hqk,qhd->khd", logit_cotangent, asking_projection_table, preferred_element_type=jnp.float32
    ).astype(jnp.bfloat16)
    dvalue = jnp.einsum(
        "hqk,qhd->khd",
        attention_weighting.astype(jnp.bfloat16),
        upstream,
        preferred_element_type=jnp.float32,
    ).astype(jnp.bfloat16)
    return (mixed_heads, dquery, grad_keys, dvalue)


def body(
    enc, dec, grad_out, w_query, w_key, w_value, w_out, enc_len, dec_len, device_perm, slot_offset
):
    here_index = lax.axis_index("dp")
    ex_count = enc_len.shape[1]
    rows_e = enc.shape[0]
    rows_d = dec.shape[0]
    head_cols = w_query.shape[1]
    heads_here = head_cols // DK
    owners = owner_table(device_perm, slot_offset, ex_count)
    enc_slots = slot_table(enc_len, rows_e)
    dec_slots = jnp.take(slot_table(dec_len, rows_d), here_index, axis=0)
    dec_f = dec.astype(jnp.float32)
    unit_dec, factor_dec = normalize(dec_f)
    normed = unit_dec.astype(jnp.bfloat16)
    q_unit, q_factor = normalize(
        jnp.dot(normed, w_query, preferred_element_type=jnp.float32).reshape(rows_d, heads_here, DK)
    )
    k_unit, k_factor = normalize(
        jnp.dot(enc, w_key, preferred_element_type=jnp.float32).reshape(rows_e, heads_here, DK)
    )
    value_flat = jnp.dot(enc, w_value, preferred_element_type=jnp.float32).astype(jnp.bfloat16)
    asking_projection_table = q_unit.astype(jnp.bfloat16)
    upstream = contract_cols(grad_out, w_out).astype(jnp.bfloat16).reshape(rows_d, heads_here, DK)
    kv_local = jnp.concatenate(
        [k_unit.astype(jnp.bfloat16).reshape(rows_e, head_cols), value_flat], axis=1
    )
    gathered = lax.all_gather(kv_local, "dp", axis=0, tiled=True)
    enc_owner = lookup(owners, enc_slots)
    key_ids = jnp.where(enc_owner == here_index, enc_slots, -1).reshape(-1)
    allowed = dec_slots[:, None] == key_ids[None, :]
    mixed_heads, dquery, grad_keys, dvalue = attend(
        asking_projection_table,
        gathered[:, :head_cols].reshape(-1, heads_here, DK),
        gathered[:, head_cols:].reshape(-1, heads_here, DK),
        upstream,
        allowed,
    )
    grads_all = jnp.concatenate(
        [grad_keys.reshape(-1, head_cols), dvalue.reshape(-1, head_cols)], axis=1
    )
    kv_grad = lax.psum_scatter(
        grads_all.astype(jnp.float32).astype(jnp.bfloat16), "dp", scatter_dimension=0, tiled=True
    )
    attended = mixed_heads.astype(jnp.bfloat16).reshape(rows_d, head_cols)
    projected = lax.psum(
        jnp.dot(attended, w_out, preferred_element_type=jnp.float32).astype(jnp.bfloat16), "mp"
    ).astype(jnp.float32)
    mixed = (dec_f + projected).astype(jnp.bfloat16)
    dk_grad = kv_grad[:, :head_cols].reshape(rows_e, heads_here, DK).astype(jnp.float32)
    key_grad_unscaled = (
        norm_back(dk_grad, k_unit, k_factor).astype(jnp.bfloat16).reshape(rows_e, head_cols)
    )
    dv_flat = kv_grad[:, head_cols:]
    dq_raw = norm_back(dquery, q_unit, q_factor).astype(jnp.bfloat16).reshape(rows_d, head_cols)
    dnormed_part = contract_cols(dq_raw, w_query)
    dnormed = lax.psum(dnormed_part.astype(jnp.bfloat16), "mp").astype(jnp.float32)
    dec_grad = (grad_out.astype(jnp.float32) + norm_back(dnormed, unit_dec, factor_dec)).astype(
        jnp.bfloat16
    )
    enc_part = contract_cols(key_grad_unscaled, w_key) + contract_cols(dv_flat, w_value)
    enc_grad = lax.psum(enc_part.astype(jnp.bfloat16), "mp")
    grad_query, grad_key, grad_value, grad_proj = (
        lax.psum_scatter(
            contract_rows(normed, dq_raw).astype(jnp.bfloat16),
            "dp",
            scatter_dimension=0,
            tiled=True,
        ).astype(jnp.float32),
        lax.psum_scatter(
            contract_rows(enc, key_grad_unscaled).astype(jnp.bfloat16),
            "dp",
            scatter_dimension=0,
            tiled=True,
        ).astype(jnp.float32),
        lax.psum_scatter(
            contract_rows(enc, dv_flat).astype(jnp.bfloat16), "dp", scatter_dimension=0, tiled=True
        ).astype(jnp.float32),
        lax.psum_scatter(
            contract_rows(attended, grad_out).astype(jnp.bfloat16),
            "dp",
            scatter_dimension=1,
            tiled=True,
        ).astype(jnp.float32),
    )
    return (mixed, dec_grad, enc_grad, grad_query, grad_key, grad_value, grad_proj)


def solution(mesh):
    in_specs = (
        P("dp", None),
        P("dp", None),
        P("dp", None),
        P(None, "mp"),
        P(None, "mp"),
        P(None, "mp"),
        P("mp", None),
        P(),
        P(),
        P(),
        P(),
    )
    out_specs = (
        P("dp", None),
        P("dp", None),
        P("dp", None),
        P("dp", "mp"),
        P("dp", "mp"),
        P("dp", "mp"),
        P("mp", "dp"),
    )
    return jax.shard_map(body, mesh=mesh, in_specs=in_specs, out_specs=out_specs, check_vma=False)
```

profile of v0, /device:TPU:0, one launch (start us, length us, event | category | flops | bytes accessed | tf_op | source)
XLA Modules:
  0.0 594.8 jit_solution(2166786573558386331)
XLA Ops:
  8.4 3.1 convolution_convert_fusion.9
  17.4 4.2 convolution_convert_fusion.8
  22.9 4.3 fusion.27
  27.2 2.2 reshape.258
  34.5 34.6 %all-gather.2.cloned.1.call-done = bf16[2048,1024]{1,0:T(8,128)(2,1)} async-done(((bf16[128,1024]{1,0:T(8,128)(2,1)}), bf16[2048,1024]{1,0:T(8,128)(2,1)}) %all-gather.2.cloned.1.call-update) | async-done | bytes 4194320 | tf_op jit(solution)/shard_map/all_gather | solution.py:128
  69.1 4.5 fusion.40
  73.6 4.0 copy.101
  77.6 3.4 convert_reduce_fusion
  81.0 2.2 convolution_convert_fusion.6
  84.8 2.6 multiply_convert_fusion
  87.4 3.9 copy.100
  91.4 3.8 convolution_convert_fusion.7
  95.2 3.9 copy.99
  99.1 4.8 pad_maximum_fusion
  104.1 3.1 multiply_reduce_fusion
  107.4 3.3 convolution_convert_fusion.3
  110.8 4.9 convolution_convert_fusion.2
  115.8 5.0 convolution_convert_fusion.4
  120.8 2.6 convolution_convert_fusion.5
  123.4 58.0 %reduce-scatter.6.cloned.1.call-done = bf16[128,1024]{1,0:T(8,128)(2,1)} async-done(((bf16[2048,1024]{1,0:T(8,128)(2,1)}), bf16[128,1024]{1,0:T(8,128)(2,1)}) %reduce-scatter.6.cloned.1.call-update) | async-done | bytes 262160 | tf_op jit(solution)/shard_map/reduce_scatter | solution.py:142
  187.8 3.7 fusion.42
  191.5 2.5 fusion.5
  194.0 3.2 fusion.4
  197.5 3.3 fusion.3
  200.8 61.4 %reduce-scatter.8.cloned.1.call-done = bf16[256,512]{1,0:T(8,128)(2,1)} async-done(((bf16[4096,512]{1,0:T(8,128)(2,1)}), bf16[256,512]{1,0:T(8,128)(2,1)}) %reduce-scatter.8.cloned.1.call-update) | async-done | bytes 262160 | tf_op jit(solution)/shard_map/reduce_scatter | solution.py:164
  264.0 78.4 %reduce-scatter.14.cloned.1.call-done = bf16[512,256]{1,0:T(8,128)(2,1)} async-done(((bf16[512,4096]{1,0:T(8,128)(2,1)}), bf16[512,256]{1,0:T(8,128)(2,1)}) %reduce-scatter.14.cloned.1.call-update) | async-done | bytes 262160 | tf_op jit(solution)/shard_map/reduce_scatter | solution.py:179
  344.2 77.7 %all-reduce.3.cloned.1.call-done = (bf16[256,4096]{1,0:T(8,128)(2,1)}, bf16[256,4096]{1,0:T(8,128)(2,1)}, bf16[128,4096]{1,0:T(8,128)(2,1)}) async-done(((bf16[256,4096]{1,0:T(8,128)(2,1)}, bf16[256,4096]{1,0:T(8,128)(2,1)}, bf16[128,4096]{1,0:T(8,128)(2,1)}), (bf16[256,4096]{1,0:T(8,128)(2,1)}, bf16[256,4096]{1,0:T(8,128)(2,1)}, bf16[128,4096]{1,0:T(8,128)(2,1)})) %all-reduce.3.cloned.1.call-update) | async-done | bytes 5242896 | tf_op jit(solution)/shard_map/psum | solution.py:146
  421.9 2.6 fusion.9
  424.7 5.9 fusion.8
  430.6 72.8 %reduce-scatter.12.cloned.1.call-done = bf16[256,512]{0,1:T(8,128)(2,1)} async-done(((bf16[4096,512]{0,1:T(8,128)(2,1)}), bf16[256,512]{0,1:T(8,128)(2,1)}) %reduce-scatter.12.cloned.1.call-update) | async-done | bytes 262160 | tf_op jit(solution)/shard_map/reduce_scatter | solution.py:176
  505.3 78.5 %reduce-scatter.10.cloned.1.call-done = bf16[256,512]{0,1:T(8,128)(2,1)} async-done(((bf16[4096,512]{0,1:T(8,128)(2,1)}), bf16[256,512]{0,1:T(8,128)(2,1)}) %reduce-scatter.10.cloned.1.call-update) | async-done | bytes 262160 | tf_op jit(solution)/shard_map/reduce_scatter | solution.py:170
  585.7 2.3 copy.122
  (96 shorter events, 29.8 us)
Async XLA Ops:
  7.2 1.2 copy-start
  7.2 61.9 %all-gather.2.cloned.1.call-start = ((), (), s32[]{:S(2)}) async-start(), calls=%async_computation.5 | async-start | bytes 4456448 | tf_op jit(solution)/shard_map/all_gather | solution.py:128
  8.4 3.4 copy-start.4
  11.8 3.1 copy-start.16
  11.8 3.2 copy-start.17
  11.9 3.4 copy-start.18
  11.9 3.5 copy-start.1
  12.8 2.5 copy-start.9
  13.3 2.1 copy-start.11
  14.9 166.6 %reduce-scatter.6.cloned.1.call-start = ((), (), s32[]{:S(2)}) async-start(), calls=%async_computation.6 | async-start | bytes 4456448 | tf_op jit(solution)/shard_map/reduce_scatter | solution.py:142
  17.3 5.2 copy-start.2
  77.6 3.4 copy-start.15
  81.0 2.2 copy-start.12
  103.9 158.3 %reduce-scatter.8.cloned.1.call-start = ((), (), s32[]{:S(2)}) async-start(), calls=%async_computation.7 | async-start | bytes 4456448 | tf_op jit(solution)/shard_map/reduce_scatter | solution.py:164
  104.1 3.1 copy-start.7
  110.7 231.7 %reduce-scatter.14.cloned.1.call-start = ((), (), s32[]{:S(2)}) async-start(), calls=%async_computation.10 | async-start | bytes 4456448 | tf_op jit(solution)/shard_map/reduce_scatter | solution.py:179
  115.7 306.1 %all-reduce.3.cloned.1.call-start = ((), (), s32[]{:S(2)}) async-start(), calls=%async_computation.11 | async-start | bytes 10485760 | tf_op jit(solution)/shard_map/psum | solution.py:146
  115.8 5.0 copy-start.8
  115.8 5.0 copy-start.14
  120.8 64.1 %copy-start.10 = (f32[128,2,256]{2,1,0:T(2,128)S(1)}, f32[128,2,256]{2,1,0:T(2,128)}, u32[]{:S(2)}) copy-start(f32[128,2,256]{2,1,0:T(2,128)} %copy-done.9) | copy-start | bytes 786436
  186.2 5.2 copy-start.3
  186.2 5.2 copy-start.13
  193.9 309.4 %reduce-scatter.12.cloned.1.call-start = ((), (), s32[]{:S(2)}) async-start(), calls=%async_computation.9 | async-start | bytes 4456448 | tf_op jit(solution)/shard_map/reduce_scatter | solution.py:176
  197.3 386.5 %reduce-scatter.10.cloned.1.call-start = ((), (), s32[]{:S(2)}) async-start(), calls=%async_computation.8 | async-start | bytes 4456448 | tf_op jit(solution)/shard_map/reduce_scatter | solution.py:170
  421.9 2.6 copy-start.5
  421.9 2.9 copy-start.6
Sparse Core Ops, SparseCore 0:
  15.0 54.1 all-gather.1
  104.0 77.3 reduce-scatter.5
  185.1 77.0 reduce-scatter.7
  265.4 77.0 reduce-scatter.13
  345.6 76.2 all-reduce.2
  425.4 77.9 reduce-scatter.11
  506.7 77.0 reduce-scatter.9
where the time goes:
time: 596 us; the launch traced here: 595 us
  waiting for transfers between devices  462 us (78%)
  matrix products  57.5 us (10%)
  local copies, waits for them, and re-layouts  33.9 us (6%)
  other arithmetic  26.7 us (4%)
  between operations  14.5 us (2%)
    reduce_scatter x1, waiting for transfers between devices, body(): lax.psum_scatter(contract_rows(enc, key_grad_unscaled).astype(jnp.bfloat1...  78.5 us
    reduce_scatter x1, waiting for transfers between devices, body(): lax.psum_scatter(contract_rows(attended, grad_out).astype(jnp.bfloat16),...  78.4 us
    psum x1, waiting for transfers between devices, body(): lax.psum(jnp.dot(attended, w_out, preferred_element_type=jnp.float32).ast...  77.7 us
    reduce_scatter x1, waiting for transfers between devices, body(): lax.psum_scatter(contract_rows(enc, dv_flat).astype(jnp.bfloat16), 'dp',...  72.8 us
    reduce_scatter x1, waiting for transfers between devices, body(): lax.psum_scatter(contract_rows(normed, dq_raw).astype(jnp.bfloat16), 'dp'...  61.4 us
    reduce_scatter x1, waiting for transfers between devices, body(): lax.psum_scatter(grads_all.astype(jnp.float32).astype(jnp.bfloat16), 'dp'...  58 us
    all_gather x1, waiting for transfers between devices, body(): gathered = lax.all_gather(kv_local, 'dp', axis=0, tiled=True)  34.6 us
    dot_general x4, matrix products, contract_cols(): lax.dot_general(former, latter, (((1,), (1,)), ((), ())), preferred_eleme...  15.3 us
  transfers between devices with their start and end apart: 7, of which 7 were waited for; matrix products, arithmetic and copies ran while one was open for 12% of the time, Pallas kernels for 0%

commit v1 on v0

v1 whole, which is shorter than its diff:
```python
import jax
import jax.numpy as jnp
from jax import lax
from jax.experimental import pallas as pl
from jax.experimental.pallas import tpu as pltpu
from jax.sharding import PartitionSpec as P

D = 4096
DK = 256
COLS = 512
DEC = 256
ENC = 128
SLOTS = 16
CAP = 16
EPS = 1e-06
SCALE = 10.0 / DK
F32 = jnp.float32
BF16 = jnp.bfloat16
MESH = pl.DeviceIdType.MESH


def dot_nn(former, latter):
    return lax.dot_general(former, latter, (((1,), (0,)), ((), ())), preferred_element_type=F32)


def dot_nt(former, latter):
    return lax.dot_general(former, latter, (((1,), (1,)), ((), ())), preferred_element_type=F32)


def rows_of(start, size):
    return pl.ds(pl.multiple_of(start, size), size)


def copy_to(src, dst, send_sem, recv_sem, device):
    return pltpu.make_async_remote_copy(
        src_ref=src,
        dst_ref=dst,
        send_sem=send_sem,
        recv_sem=recv_sem,
        device_id=device,
        device_id_type=MESH,
    )


def partners(place, core):
    one = place + 1 - 2 * lax.rem(place, 2)
    three = 3 - place
    first = one + core * (three - one)
    second = three + core * (one - three)
    return first, second, lax.rem(place + 2, 4)


class Spread:
    def __init__(self, at, source, target, send, recv):
        self.at, self.source, self.target, self.send, self.recv = at, source, target, send, recv
        self.rows = target.shape[1] // 8
        self.sent = []

    def chunk(self, y):
        return self.target.at[:, rows_of((self.at.c * 4 + y) * self.rows, self.rows), :]

    def go(self, src, dst, index, device):
        copy = copy_to(src, dst, self.send.at[index], self.recv.at[index], device)
        copy.start()
        self.sent.append(copy)

    def wait(self, ref, index):
        copy_to(ref, ref, self.send.at[index], self.recv.at[index], self.at.other_core).wait_recv()

    def over_x(self):
        at = self.at
        mine = rows_of((at.c * 4 + at.y) * self.rows, self.rows)
        for off in (1, 3, 2):
            x = lax.rem(at.x + off, 4)
            self.go(
                self.source.at[mine, rows_of(x * 1024, 1024)],
                self.target.at[3 - off, mine, :],
                3 - off,
                (x * 4 + at.z, at.mp),
            )

    def over_y(self):
        at = self.at
        mine = rows_of((at.c * 4 + at.y) * self.rows, self.rows)
        for place in range(3):
            self.wait(self.target.at[place, mine, :], place)
        self.go(self.chunk(at.y), self.chunk(at.y), 3, at.y_dev(at.ya))
        self.go(self.chunk(at.y), self.chunk(at.y), 4, at.y_dev(at.yb))

    def over_y_again(self):
        at = self.at
        self.wait(self.chunk(at.ya), 3)
        self.go(self.chunk(at.ya), self.chunk(at.ya), 5, at.y_dev(at.yb))

    def over_core(self):
        at = self.at
        self.wait(self.chunk(at.yb), 4)
        self.wait(self.chunk(at.y2), 5)
        half = self.target.at[:, rows_of(at.c * 4 * self.rows, 4 * self.rows), :]
        self.go(half, half, 6, at.other_core)

    def finish(self):
        at = self.at
        half = self.target.at[:, rows_of((1 - at.c) * 4 * self.rows, 4 * self.rows), :]
        self.wait(half, 6)


class Summed:
    def __init__(self, at, part, core_in, y_in, final, out, send, recv, local):
        self.at, self.part, self.core_in, self.y_in = at, part, core_in, y_in
        self.final, self.out, self.send, self.recv, self.local = final, out, send, recv, local
        self.half = part.shape[0] // 2
        self.rows = part.shape[0] // 8
        self.sent = []

    def go(self, src, dst, index, device):
        copy = copy_to(src, dst, self.send.at[index], self.recv.at[index], device)
        copy.start()
        self.sent.append(copy)

    def wait(self, ref, index):
        copy_to(ref, ref, self.send.at[index], self.recv.at[index], self.at.other_core).wait_recv()

    def rows_at(self, y, core=None):
        core = self.at.c if core is None else core
        return rows_of((core * 4 + y) * self.rows, self.rows)

    def over_core(self):
        other = 1 - self.at.c
        self.go(self.part.at[rows_of(other * self.half, self.half)], self.core_in, 0, self.at.other_core)

    def add_core(self, y):
        rows = self.rows_at(y)
        got = self.core_in[rows_of(y * self.rows, self.rows), :]
        self.part[rows, :] = (self.part[rows, :].astype(F32) + got.astype(F32)).astype(BF16)

    def first(self):
        at = self.at
        self.wait(self.core_in, 0)
        self.add_core(at.y2)
        self.go(self.part.at[self.rows_at(at.y2)], self.y_in.at[0], 1, at.y_dev(at.ya))
        self.add_core(at.ya)
        self.go(self.part.at[self.rows_at(at.ya)], self.y_in.at[1], 2, at.y_dev(at.ya))
        self.add_core(at.yb)
        self.add_core(at.y)

    def second(self):
        at = self.at
        self.wait(self.y_in.at[0], 1)
        rows = self.rows_at(at.yb)
        self.part[rows, :] = (self.part[rows, :].astype(F32) + self.y_in[0].astype(F32)).astype(BF16)
        self.go(self.part.at[rows], self.y_in.at[2], 3, at.y_dev(at.yb))

    def total(self):
        self.wait(self.y_in.at[1], 2)
        self.wait(self.y_in.at[2], 3)
        rows = self.rows_at(self.at.y)
        return self.part[rows, :].astype(F32) + self.y_in[1].astype(F32) + self.y_in[2].astype(F32)

    def share(self):
        at = self.at
        rows = self.rows_at(at.y)
        self.go(self.final, self.out.at[rows], 4, at.y_dev(at.ya))
        self.go(self.final, self.out.at[rows], 5, at.y_dev(at.yb))
        self.go(self.final, self.out.at[rows], 7, at.other_core)
        pltpu.make_async_copy(self.final, self.out.at[rows], self.local).start()

    def forward(self):
        at = self.at
        rows = self.out.at[self.rows_at(at.ya)]
        self.wait(rows, 4)
        self.go(rows, rows, 6, at.y_dev(at.yb))
        self.go(rows, rows, 8, at.other_core)
        rows = self.out.at[self.rows_at(at.yb)]
        self.wait(rows, 5)
        self.go(rows, rows, 9, at.other_core)

    def forward_last(self):
        rows = self.out.at[self.rows_at(self.at.y2)]
        self.wait(rows, 6)
        self.go(rows, rows, 10, self.at.other_core)

    def finish(self):
        at = self.at
        other = 1 - at.c
        for index, y in ((7, at.y), (8, at.yb), (9, at.ya), (10, at.y2)):
            self.wait(self.out.at[self.rows_at(y, other)], index)
        pltpu.make_async_copy(self.final, self.out.at[self.rows_at(at.y)], self.local).wait()


class Weight:
    def __init__(self, at, factor, part, z_in, send, recv):
        self.at, self.factor, self.part, self.z_in = at, factor, part, z_in
        self.send, self.recv = send, recv
        self.sent = []

    def go(self, src, dst, index, device):
        copy = copy_to(src, dst, self.send.at[index], self.recv.at[index], device)
        copy.start()
        self.sent.append(copy)

    def wait(self, ref, index):
        copy_to(ref, ref, self.send.at[index], self.recv.at[index], self.at.other_core).wait_recv()

    def gather(self):
        at = self.at
        mine = self.factor.at[at.x]
        self.go(mine, mine, 0, at.x_dev(at.xa))
        self.go(mine, mine, 1, at.x_dev(at.xb))

    def gather_again(self):
        at = self.at
        theirs = self.factor.at[at.xa]
        self.wait(theirs, 0)
        self.go(theirs, theirs, 2, at.x_dev(at.xb))

    def gathered(self):
        at = self.at
        self.wait(self.factor.at[at.xb], 1)
        self.wait(self.factor.at[at.x2], 2)

    def block(self, z, own, spread):
        at = self.at
        total = dot_nn(self.factor[at.x], own[:, rows_of(at.x * 1024 + z * 256, 256)])
        for place in range(3):
            peer = lax.rem(at.x + 1 + place, 4)
            total += dot_nn(self.factor[peer], spread[place, :, rows_of(z * 256, 256)])
        self.part[z] = total.astype(BF16)

    def product(self, own, spread):
        at = self.at
        self.block(at.z2, own, spread)
        self.go(self.part.at[at.z2], self.z_in.at[0], 3, at.z_dev(at.za))
        self.block(at.za, own, spread)
        self.go(self.part.at[at.za], self.z_in.at[1], 4, at.z_dev(at.za))
        self.block(at.zb, own, spread)
        self.block(at.z, own, spread)

    def second(self):
        at = self.at
        self.wait(self.z_in.at[0], 3)
        self.part[at.zb] = (self.part[at.zb].astype(F32) + self.z_in[0].astype(F32)).astype(BF16)
        self.go(self.part.at[at.zb], self.z_in.at[2], 5, at.z_dev(at.zb))

    def total(self):
        self.wait(self.z_in.at[1], 4)
        self.wait(self.z_in.at[2], 5)
        return self.part[self.at.z].astype(F32) + self.z_in[1].astype(F32) + self.z_in[2].astype(F32)


class Place:
    def __init__(self):
        self.dp = lax.axis_index("dp")
        self.mp = lax.axis_index("mp")
        self.x, self.z = lax.div(self.dp, 4), lax.rem(self.dp, 4)
        self.y, self.c = lax.div(self.mp, 2), lax.rem(self.mp, 2)
        self.xa, self.xb, self.x2 = partners(self.x, self.c)
        self.ya, self.yb, self.y2 = partners(self.y, self.c)
        self.za, self.zb, self.z2 = partners(self.z, self.c)
        self.other_core = (self.dp, self.y * 2 + 1 - self.c)

    def x_dev(self, x):
        return (x * 4 + self.z, self.mp)

    def y_dev(self, y):
        return (self.dp, y * 2 + self.c)

    def z_dev(self, z):
        return (self.x * 4 + z, self.mp)


def head(h):
    return slice(h * DK, (h + 1) * DK)


def unit_heads(raw, unit, factor):
    for h in range(2):
        rows = raw[:, head(h)]
        inverse = lax.rsqrt(jnp.mean(rows * rows, axis=1, keepdims=True) + EPS)
        unit[:, head(h)] = rows * inverse
        factor[h] = jnp.broadcast_to(inverse, factor.shape[1:])


def head_back(upstream, unit, factor, h):
    rows = unit[:, head(h)]
    mean = jnp.mean(upstream * rows, axis=1, keepdims=True)
    return factor[h][:, :1] * (upstream - rows * mean)


def kernel(
    enc_h, dec_h, go_h, wq_h, wk_h, wv_h, wo_h, pack_ref, unpack_ref, mask_ref,
    mixed_h, decg_h, encg_h, gq_h, gk_h, gv_h, gp_h,
    enc, dec, go, wq, wk, wv, wo,
    xdec, xgo, xenc,
    raw_d, raw_e, qu, qa, ku, kb, r_dec, qb, up, kv, kv_out, kv_in, g_out, g_in, probs, att, dqb, dkb, dvb,
    p_mix, c_mix, y_mix, f_mix, p_dec, c_dec, y_dec, f_dec, p_enc, c_enc, y_enc, f_enc,
    fq, fk, fv, fp, pq, pk, pv, pp, zq, zk, zv, zp, oq, ok, ov, op,
    load_sem, kv_send, kv_recv, g_send, g_recv, x_send, x_recv, s_send, s_recv, s_local, w_send, w_recv, w_local,
):
    at = Place()

    loads = []
    for src, dst in (
        (enc_h, enc), (wk_h, wk), (wv_h, wv), (dec_h, dec), (wq_h, wq), (go_h, go), (wo_h, wo),
    ):
        copy = pltpu.make_async_copy(src, dst, load_sem.at[len(loads)])
        copy.start()
        loads.append(copy)
    l_enc, l_wk, l_wv, l_dec, l_wq, l_go, l_wo = loads

    barrier = pltpu.get_barrier_semaphore()

    @pl.loop(1, 16)
    def _(off):
        pl.semaphore_signal(
            barrier, inc=1, device_id=(lax.rem(at.dp + off, 16), at.mp), device_id_type=MESH
        )

    for device in (at.other_core, at.y_dev(at.ya), at.y_dev(at.yb)):
        pl.semaphore_signal(barrier, inc=1, device_id=device, device_id_type=MESH)
    pl.semaphore_wait(barrier, 18)

    s_dec = Spread(at, dec_h, xdec, x_send.at[0], x_recv.at[0])
    s_go = Spread(at, go_h, xgo, x_send.at[1], x_recv.at[1])
    s_enc = Spread(at, enc_h, xenc, x_send.at[2], x_recv.at[2])
    spreads = (s_go, s_dec, s_enc)
    for spread in spreads:
        spread.over_x()

    def project(total, rows, weight):
        total[...] = jnp.zeros_like(total)

        @pl.loop(0, 4)
        def _(k):
            cols = rows_of(k * 1024, 1024)
            total[...] += dot_nn(rows[:, cols], weight[cols, :])

    l_enc.wait()
    l_wk.wait()
    project(raw_e, enc, wk)
    unit_heads(raw_e, ku, kb)
    kv[:, :COLS] = ku[...].astype(BF16)
    l_wv.wait()
    project(raw_e, enc, wv)
    kv[:, COLS:] = raw_e[...].astype(BF16)
    for half in range(2):
        cols = slice(half * COLS, (half + 1) * COLS)
        kv_out[:, cols] = dot_nn(pack_ref[...], kv[:, cols]).astype(BF16)

    def exchange(source, target, send, recv):
        @pl.loop(1, 16)
        def _(off):
            peer = lax.rem(at.dp + off, 16)
            copy_to(
                source.at[rows_of(peer * CAP, CAP)],
                target.at[rows_of(at.dp * CAP, CAP)],
                send.at[peer],
                recv.at[at.dp],
                (peer, at.mp),
            ).start()

        mine = rows_of(at.dp * CAP, CAP)
        target[mine, :] = source[mine, :]

    def exchanged(source, target, send, recv):
        @pl.loop(1, 16)
        def _(off):
            peer = lax.rem(at.dp + off, 16)
            block = rows_of(peer * CAP, CAP)
            copy_to(source.at[block], target.at[block], send.at[peer], recv.at[peer], (peer, at.mp)).wait()

    exchange(kv_out, kv_in, kv_send, kv_recv)

    for spread in spreads:
        spread.over_y()
    l_dec.wait()
    raw_d[...] = jnp.zeros_like(raw_d)

    @pl.loop(0, 8)
    def _(k):
        rows = dec[:, rows_of(k * COLS, COLS)].astype(F32)
        raw_d[...] += rows * rows

    r_dec[...] = jnp.broadcast_to(
        lax.rsqrt(jnp.sum(raw_d[...], axis=1, keepdims=True) * (1.0 / D) + EPS), r_dec.shape
    )
    l_wq.wait()
    raw_d[...] = jnp.zeros_like(raw_d)

    @pl.loop(0, 4)
    def _(k):
        cols = rows_of(k * 1024, 1024)
        normed = (dec[:, cols].astype(F32) * r_dec[:, :1]).astype(BF16)
        raw_d[...] += dot_nn(normed, wq[cols, :])

    unit_heads(raw_d, qu, qa)
    qb[...] = qu[...].astype(BF16)

    for spread in spreads:
        spread.over_y_again()
    l_go.wait()
    l_wo.wait()
    raw_d[...] = jnp.zeros_like(raw_d)

    @pl.loop(0, 4)
    def _(k):
        cols = rows_of(k * 1024, 1024)
        raw_d[...] += dot_nt(go[:, cols], wo[:, cols])

    up[...] = raw_d[...].astype(BF16)
    for spread in spreads:
        spread.over_core()

    grad_q = Weight(at, fq, pq, zq, w_send.at[0], w_recv.at[0])
    grad_k = Weight(at, fk, pk, zk, w_send.at[1], w_recv.at[1])
    grad_v = Weight(at, fv, pv, zv, w_send.at[2], w_recv.at[2])
    grad_p = Weight(at, fp, pp, zp, w_send.at[3], w_recv.at[3])
    s_mix = Summed(at, p_mix, c_mix, y_mix, f_mix, mixed_h, s_send.at[0], s_recv.at[0], s_local.at[0])
    s_dng = Summed(at, p_dec, c_dec, y_dec, f_dec, decg_h, s_send.at[1], s_recv.at[1], s_local.at[1])
    s_eng = Summed(at, p_enc, c_enc, y_enc, f_enc, encg_h, s_send.at[2], s_recv.at[2], s_local.at[2])

    exchanged(kv_out, kv_in, kv_send, kv_recv)
    for h in range(2):
        keys, values = kv_in[:, head(h)], kv_in[:, head(h + 2)]
        scores = dot_nt(qb[:, head(h)], keys) * SCALE
        weights = jnp.where(mask_ref[...] > 0.0, jnp.exp(scores), 0.0).astype(BF16)
        wide = weights.astype(F32)
        totals = jnp.sum(wide, axis=1, keepdims=True)
        probs[h] = wide / totals
        heads_out = dot_nn(weights, values) / totals
        raw_d[:, head(h)] = heads_out
        att[:, head(h)] = heads_out.astype(BF16)
        fp[at.x, head(h), :] = heads_out.T.astype(BF16)
    grad_p.gather()

    def mix(half):
        rows = rows_of(half * 128, 128)

        @pl.loop(0, 4)
        def _(k):
            cols = rows_of(k * 1024, 1024)
            p_mix[rows, cols] = dot_nn(att[rows, :], wo[:, cols]).astype(BF16)

    mix(1 - at.c)
    s_mix.over_core()
    mix(at.c)

    for h in range(2):
        keys, values = kv_in[:, head(h)], kv_in[:, head(h + 2)]
        upstream = up[:, head(h)]
        weighting = probs[h]
        delta = jnp.sum(upstream.astype(F32) * raw_d[:, head(h)], axis=1, keepdims=True)
        dscore = weighting * (dot_nt(upstream, values) - delta) * SCALE
        g_out[:, head(h)] = dot_nn(dscore.T.astype(BF16), qb[:, head(h)]).astype(BF16)
        g_out[:, head(h + 2)] = dot_nn(weighting.T.astype(BF16), upstream).astype(BF16)
        dquery = dot_nn(dscore.astype(BF16), keys)
        dq_raw = head_back(dquery, qu, qa, h)
        dqb[:, head(h)] = dq_raw.astype(BF16)
        fq[at.x, head(h), :] = (dq_raw * r_dec[:, :1]).T.astype(BF16)
    exchange(g_out, g_in, g_send, g_recv)
    grad_q.gather()
    s_mix.first()

    def dnormed(half):
        rows = rows_of(half * 128, 128)

        @pl.loop(0, 4)
        def _(k):
            cols = rows_of(k * 1024, 1024)
            p_dec[rows, cols] = dot_nt(dqb[rows, :], wq[cols, :]).astype(BF16)

    dnormed(1 - at.c)
    s_dng.over_core()
    dnormed(at.c)
    grad_p.gather_again()
    s_mix.second()

    exchanged(g_out, g_in, g_send, g_recv)
    for h in range(2):
        dkey = dot_nn(unpack_ref[...], g_in[:, head(h)])
        dk_raw = head_back(dkey, ku, kb, h)
        dkb[:, head(h)] = dk_raw.astype(BF16)
        fk[at.x, head(h), :] = dk_raw.T.astype(BF16)
        dvalue = dot_nn(unpack_ref[...], g_in[:, head(h + 2)])
        dvb[:, head(h)] = dvalue.astype(BF16)
        fv[at.x, head(h), :] = dvalue.T.astype(BF16)
    grad_k.gather()
    grad_v.gather()
    grad_q.gather_again()
    s_dng.first()

    @pl.loop(0, 4)
    def _(k):
        cols = rows_of(k * 1024, 1024)
        p_enc[:, cols] = (dot_nt(dkb[...], wk[cols, :]) + dot_nt(dvb[...], wv[cols, :])).astype(BF16)

    s_eng.over_core()

    mine_d = rows_of((at.c * 4 + at.y) * 32, 32)
    f_mix[...] = (dec[mine_d, :].astype(F32) + s_mix.total()).astype(BF16)
    s_mix.share()

    s_go.finish()
    grad_p.gathered()
    grad_p.product(go, xgo)
    s_dng.second()
    s_eng.first()
    grad_k.gather_again()
    grad_v.gather_again()
    s_mix.forward()

    s_dec.finish()
    grad_q.gathered()
    grad_q.product(dec, xdec)
    s_eng.second()
    grad_p.second()

    total = s_dng.total()
    unit = dec[mine_d, :].astype(F32) * r_dec[mine_d, :1]
    mean = jnp.mean(total * unit, axis=1, keepdims=True)
    back = r_dec[mine_d, :1] * (total - unit * mean)
    f_dec[...] = (go[mine_d, :].astype(F32) + back).astype(BF16)
    s_dng.share()
    s_mix.forward_last()

    s_enc.finish()
    grad_k.gathered()
    grad_k.product(enc, xenc)
    grad_v.gathered()
    grad_v.product(enc, xenc)
    f_enc[...] = s_eng.total().astype(BF16)
    s_eng.share()
    grad_q.second()
    s_dng.forward()

    outs = []

    def store(source, target):
        copy = pltpu.make_async_copy(source, target, w_local.at[len(outs)])
        copy.start()
        outs.append(copy)

    op[...] = grad_p.total()
    store(op, gp_h)
    grad_k.second()
    grad_v.second()
    s_eng.forward()
    s_dng.forward_last()
    oq[...] = grad_q.total().T
    store(oq, gq_h)
    ok[...] = grad_k.total().T
    store(ok, gk_h)
    ov[...] = grad_v.total().T
    store(ov, gv_h)
    s_eng.forward_last()
    for summed in (s_mix, s_dng, s_eng):
        summed.finish()
    for copy in outs:
        copy.wait()
    for user in (*spreads, s_mix, s_dng, s_eng, grad_q, grad_k, grad_v, grad_p):
        for copy in user.sent:
            copy.wait_send()


def tables(enc_len, dec_len, device_perm, slot_offset):
    here = lax.axis_index("dp")
    slots = jnp.arange(SLOTS, dtype=jnp.int32)
    owners = jnp.take(device_perm, (slots[:, None] + slot_offset[None, :]) % SLOTS, axis=0)

    def placed(lengths, rows):
        ends = jnp.cumsum(lax.dynamic_index_in_dim(lengths, here, 0, False), dtype=jnp.int32)
        past = jnp.arange(rows, dtype=jnp.int32)[:, None] >= ends[None, :]
        slot = jnp.sum(past.astype(jnp.int32), axis=1)
        return slot, jnp.max(jnp.where(past, ends[None, :], 0), axis=1)

    slot, start = placed(enc_len, ENC)
    mine = lax.dynamic_index_in_dim(owners, here, 0, False)
    owner = jnp.sum(jnp.where(slot[:, None] == slots[None, :], mine[None, :], 0), axis=1)
    target = owner * CAP + jnp.arange(ENC, dtype=jnp.int32) - start
    pack = jnp.arange(SLOTS * CAP, dtype=jnp.int32)[:, None] == target[None, :]
    unpack = target[:, None] == jnp.arange(SLOTS * CAP, dtype=jnp.int32)[None, :]

    chosen = owners == here
    key_slot = jnp.sum(jnp.where(chosen, slots[None, :], 0), axis=1)
    key_len = jnp.sum(jnp.where(chosen, enc_len, 0), axis=1)
    key_id = jnp.where(slots[None, :] < key_len[:, None], key_slot[:, None], -1).reshape(-1)
    dec_slot, _ = placed(dec_len, DEC)
    mask = dec_slot[:, None] == key_id[None, :]
    return pack.astype(BF16), unpack.astype(BF16), mask.astype(F32)


def body(enc, dec, grad_out, w_query, w_key, w_value, w_out, enc_len, dec_len, device_perm, slot_offset):
    pack, unpack, mask = tables(enc_len, dec_len, device_perm, slot_offset)
    anywhere = pl.BlockSpec(memory_space=pl.ANY)
    whole = pl.BlockSpec(memory_space=pltpu.VMEM)
    vmem = pltpu.VMEM
    dma = pltpu.SemaphoreType.DMA
    scratch = [
        vmem((ENC, D), BF16), vmem((DEC, D), BF16), vmem((DEC, D), BF16),
        vmem((D, COLS), BF16), vmem((D, COLS), BF16), vmem((D, COLS), BF16), vmem((COLS, D), BF16),
        vmem((3, DEC, 1024), BF16), vmem((3, DEC, 1024), BF16), vmem((3, ENC, 1024), BF16),
        vmem((DEC, COLS), F32), vmem((ENC, COLS), F32),
        vmem((DEC, COLS), F32), vmem((2, DEC, 128), F32),
        vmem((ENC, COLS), F32), vmem((2, ENC, 128), F32),
        vmem((DEC, 128), F32), vmem((DEC, COLS), BF16), vmem((DEC, COLS), BF16),
        vmem((ENC, 2 * COLS), BF16),
        vmem((256, 2 * COLS), BF16), vmem((256, 2 * COLS), BF16),
        vmem((256, 2 * COLS), BF16), vmem((256, 2 * COLS), BF16),
        vmem((2, DEC, 256), F32), vmem((DEC, COLS), BF16), vmem((DEC, COLS), BF16),
        vmem((ENC, COLS), BF16), vmem((ENC, COLS), BF16),
    ]
    for rows in (DEC, DEC, ENC):
        scratch += [
            vmem((rows, D), BF16), vmem((rows // 2, D), BF16),
            vmem((3, rows // 8, D), BF16), vmem((rows // 8, D), BF16),
        ]
    scratch += [vmem((4, COLS, rows), BF16) for rows in (DEC, ENC, ENC, DEC)]
    scratch += [vmem((4, COLS, 256), BF16)] * 4
    scratch += [vmem((3, COLS, 256), BF16)] * 4
    scratch += [vmem((256, COLS), F32)] * 3 + [vmem((COLS, 256), F32)]
    scratch += [
        dma((7,)), dma((16,)), dma((16,)), dma((16,)), dma((16,)),
        dma((3, 7)), dma((3, 7)), dma((3, 11)), dma((3, 11)), dma((3,)),
        dma((4, 6)), dma((4, 6)), dma((4,)),
    ]
    return pl.pallas_call(
        kernel,
        out_shape=(
            jax.ShapeDtypeStruct((DEC, D), BF16),
            jax.ShapeDtypeStruct((DEC, D), BF16),
            jax.ShapeDtypeStruct((ENC, D), BF16),
            jax.ShapeDtypeStruct((256, COLS), F32),
            jax.ShapeDtypeStruct((256, COLS), F32),
            jax.ShapeDtypeStruct((256, COLS), F32),
            jax.ShapeDtypeStruct((COLS, 256), F32),
        ),
        in_specs=[anywhere] * 7 + [whole] * 3,
        out_specs=[anywhere] * 7,
        scratch_shapes=scratch,
        compiler_params=pltpu.CompilerParams(
            collective_id=0, has_side_effects=True, vmem_limit_bytes=60 * 1024 * 1024
        ),
        name="cross_attention",
    )(enc, dec, grad_out, w_query, w_key, w_value, w_out, pack, unpack, mask)


def solution(mesh):
    in_specs = (
        P("dp", None), P("dp", None), P("dp", None),
        P(None, "mp"), P(None, "mp"), P(None, "mp"), P("mp", None),
        P(), P(), P(), P(),
    )
    out_specs = (
        P("dp", None), P("dp", None), P("dp", None),
        P("dp", "mp"), P("dp", "mp"), P("dp", "mp"), P("mp", "dp"),
    )
    return jax.shard_map(body, mesh=mesh, in_specs=in_specs, out_specs=out_specs, check_vma=False)
```

time: 596 us -> 123 us (0.21)
  waiting for transfers between devices: 462 us -> 0 us
  Pallas kernels: 0 us -> 104 us
  matrix products: 57.5 us -> 0 us
  other arithmetic: 26.7 us -> 3.64 us
  local copies, waits for them, and re-layouts: 33.9 us -> 12.8 us
  between operations: 14.5 us -> 0.73 us
    reduce_scatter x5 -> x0, waiting for transfers between devices: 349 us -> none  [the longest x1 78.5 us: body(): lax.psum_scatter(contract_rows(enc, key_grad_unscaled).astype(jnp.bfloat1...]
    pallas_call x0 -> x1, Pallas kernels: none -> 104 us  [body(): pl.pallas_call(kernel, out_shape=(jax.ShapeDtypeStruct((DEC, D), BF16), j...]
    psum x1 -> x0, waiting for transfers between devices: 77.7 us -> none  [body(): lax.psum(jnp.dot(attended, w_out, preferred_element_type=jnp.float32).ast...]
    dot_general x18 -> x0, matrix products: 57.5 us -> none  [the longest x4 15.3 us: contract_cols(): lax.dot_general(former, latter, (((1,), (1,)), ((), ())), preferred_eleme...]
    all_gather x1 -> x0, waiting for transfers between devices: 34.6 us -> none  [body(): gathered = lax.all_gather(kv_local, 'dp', axis=0, tiled=True)]
    reshape x6 -> x0, local copies, waits for them, and re-layouts: 16.2 us -> none  [the longest x2 4.2 us: body(): jnp.dot(normed, w_query, preferred_element_type=jnp.float32)]
    convert_element_type x7 -> x3, other arithmetic: 13.2 us -> 2.17 us  [tables(): return (pack.astype(BF16), unpack.astype(BF16), mask.astype(F32))]
    reduce_sum x8 -> x4, other arithmetic: 6.34 us -> 0.38 us  [the longest x2 0.18 us: placed(): slot = jnp.sum(past.astype(jnp.int32), axis=1)]
  transfers between devices with their start and end apart: 7 -> 0, of which waited for: 7 -> 0; matrix products, arithmetic and copies ran while one was open for 12% -> 0% of each run, Pallas kernels for 0% -> 0%
where the time goes in v1:
time: 123 us; the launch traced here: 122 us
  Pallas kernels  104 us (85%)
  local copies, waits for them, and re-layouts  12.8 us (10%)
  other arithmetic  3.64 us (3%)
    pallas_call x1, Pallas kernels, body(): pl.pallas_call(kernel, out_shape=(jax.ShapeDtypeStruct((DEC, D), BF16), j...  104 us
    unnamed x25, local copies, waits for them, and re-layouts  9.81 us

profile of v1, /device:TPU:0, one launch (start us, length us, event | category | flops | bytes accessed | tf_op | source)
XLA Modules:
  0.0 121.6 jit_solution(17401273362132761211)
XLA Ops:
  0.6 0.0 copy-start
  0.7 0.7 fusion.11
  1.4 0.1 copy.22
  1.5 0.1 reduce
  1.6 0.1 convert_reduce_fusion.1
  1.7 0.1 copy.23
  1.8 0.1 reduce.1
  1.9 0.1 convert_reduce_fusion
  2.0 0.7 compare_select_fusion
  2.7 0.1 reshape.200
  2.8 0.0 copy-done
  2.8 0.0 copy-start.8
  2.8 0.0 copy-start.7
  2.8 1.9 %gather_fusion = s32[256]{0:T(256)S(1)} fusion(s32[16]{0:T(128)S(1)} %copy-done, s32[1024]{0:T(1024)S(1)} %pad_clamp_fusion), kind=kCustom, calls=%fused_computation | custom fusion | bytes 3072 | tf_op jit(solution)/shard_map/jit(_take)/gather | solution.py:568
  4.7 0.1 reshape.199
  4.8 0.1 select_reduce_fusion.1
  4.9 0.1 select_reduce_fusion.3
  5.0 0.1 fusion.10
  5.1 0.1 select_n.81
  5.2 0.7 fusion.1.unpack_ref
  5.9 0.6 fusion.pack_ref
  6.6 0.8 compare_convert_fusion.mask_ref
  7.4 104.4 %cross_attention.1 = (bf16[256,4096]{1,0:T(8,128)(2,1)}, bf16[256,4096]{1,0:T(8,128)(2,1)}, bf16[128,4096]{1,0:T(8,128)(2,1)}, f32[256,512]{1,0:T(8,128)}, f32[2...) custom-call(bf16[128,4096]{1,0:T(8,128)(2,1)} %enc_h.1, bf16[256,4096]{1,0:T(8,128)(2,1)} %dec_h.1, ...), custom_call_target="tpu_custom_call" | custom-call | tf_op jit(solution)/shard_map/cross_attention/pallas_call | solution.py:626
  111.8 3.3 %copy.31 = bf16[256,4096]{1,0:T(8,128)(2,1)} copy(bf16[256,4096]{1,0:T(8,128)(2,1)} %get-tuple-element.22) | data formatting | bytes 4194304
  115.1 1.3 %copy.32 = bf16[256,4096]{1,0:T(8,128)(2,1)} copy(bf16[256,4096]{1,0:T(8,128)(2,1)S(1)} %copy-done.1) | data formatting | bytes 4194304
  116.4 0.6 copy-done.2
  117.0 1.0 copy.33
  118.0 0.4 copy-done.6
  118.4 0.8 copy.34
  119.2 0.8 copy.35
  120.0 0.8 copy.36
  120.8 0.8 copy.37
  (18 shorter events, 0.1 us)
Async XLA Ops:
  0.6 2.2 %copy-start = (s32[16]{0:T(128)S(1)}, s32[16]{0:T(128)}, u32[]{:S(2)}) copy-start(s32[16]{0:T(128)} %param.20) | copy-start | bytes 196
  2.8 2.0 %copy-start.8 = (s32[16]{0:T(128)S(1)}, s32[16]{0:T(128)}, u32[]{:S(2)}) copy-start(s32[16]{0:T(128)} %param.21) | copy-start | bytes 196
  2.8 2.0 %copy-start.7 = (s32[16,16]{1,0:T(8,128)S(1)}, s32[16,16]{1,0:T(8,128)}, u32[]{:S(2)}) copy-start(s32[16,16]{1,0:T(8,128)} %param.18) | copy-start | bytes 3076
  111.8 3.3 %copy-start.1 = (bf16[256,4096]{1,0:T(8,128)(2,1)S(1)}, bf16[256,4096]{1,0:T(8,128)(2,1)}, u32[]{:S(2)}) copy-start(bf16[256,4096]{1,0:T(8,128)(2,1)} %get-tuple-element.23) | copy-start | bytes 6291460
  115.1 2.0 %copy-start.2 = (bf16[128,4096]{1,0:T(8,128)(2,1)S(1)}, bf16[128,4096]{1,0:T(8,128)(2,1)}, u32[]{:S(2)}) copy-start(bf16[128,4096]{1,0:T(8,128)(2,1)} %get-tuple-element.24) | copy-start | bytes 3145732
  117.0 1.4 %copy-start.6 = (f32[256,512]{1,0:T(8,128)S(1)}, f32[256,512]{1,0:T(8,128)}, u32[]{:S(2)}) copy-start(f32[256,512]{1,0:T(8,128)} %get-tuple-element.25) | copy-start | bytes 1572868
  117.0 2.2 %copy-start.5 = (f32[256,512]{1,0:T(8,128)S(1)}, f32[256,512]{1,0:T(8,128)}, u32[]{:S(2)}) copy-start(f32[256,512]{1,0:T(8,128)} %get-tuple-element.26) | copy-start | bytes 1572868
  117.0 3.0 %copy-start.4 = (f32[256,512]{1,0:T(8,128)S(1)}, f32[256,512]{1,0:T(8,128)}, u32[]{:S(2)}) copy-start(f32[256,512]{1,0:T(8,128)} %get-tuple-element.27) | copy-start | bytes 1572868
  118.4 2.4 %copy-start.3 = (f32[512,256]{1,0:T(8,128)S(1)}, f32[512,256]{1,0:T(8,128)}, u32[]{:S(2)}) copy-start(f32[512,256]{1,0:T(8,128)} %get-tuple-element.28) | copy-start | bytes 1572868

commit v2 on v1

--- a/solution.py
+++ b/solution.py
@@ -50,9 +50,18 @@
     return first, second, lax.rem(place + 2, 4)
 
 
+class Line:
+    def __init__(self, me, core, device, own_step, other_step):
+        self.me, self.device, self.own_step, self.other_step = me, device, own_step, other_step
+        self.a, self.b, self.far = partners(me, core)
+
+    def column(self, own, other):
+        return own * self.own_step + other * self.other_step
+
+
 class Spread:
-    def __init__(self, at, source, target, send, recv):
-        self.at, self.source, self.target, self.send, self.recv = at, source, target, send, recv
+    def __init__(self, at, line, source, target, send, recv):
+        self.at, self.line, self.source, self.target, self.send, self.recv = at, line, source, target, send, recv
         self.rows = target.shape[1] // 8
         self.sent = []
 
@@ -67,23 +76,31 @@
     def wait(self, ref, index):
         copy_to(ref, ref, self.send.at[index], self.recv.at[index], self.at.other_core).wait_recv()
 
-    def over_x(self):
-        at = self.at
+    def blocks(self, place):
+        if self.line.own_step == 1024:
+            return [(place, slice(0, 1024), 0)]
+        return [(7 + place * 4 + j, slice(j * 256, (j + 1) * 256), j) for j in range(4)]
+
+    def over_line(self):
+        at, line = self.at, self.line
         mine = rows_of((at.c * 4 + at.y) * self.rows, self.rows)
         for off in (1, 3, 2):
-            x = lax.rem(at.x + off, 4)
-            self.go(
-                self.source.at[mine, rows_of(x * 1024, 1024)],
-                self.target.at[3 - off, mine, :],
-                3 - off,
-                (x * 4 + at.z, at.mp),
-            )
+            peer = lax.rem(line.me + off, 4)
+            for index, cols, j in self.blocks(3 - off):
+                width = cols.stop - cols.start
+                self.go(
+                    self.source.at[mine, rows_of(line.column(peer, j), width)],
+                    self.target.at[3 - off, mine, cols],
+                    index,
+                    line.device(peer),
+                )
 
     def over_y(self):
         at = self.at
         mine = rows_of((at.c * 4 + at.y) * self.rows, self.rows)
         for place in range(3):
-            self.wait(self.target.at[place, mine, :], place)
+            for index, cols, _ in self.blocks(place):
+                self.wait(self.target.at[place, mine, cols], index)
         self.go(self.chunk(at.y), self.chunk(at.y), 3, at.y_dev(at.ya))
         self.go(self.chunk(at.y), self.chunk(at.y), 4, at.y_dev(at.yb))
 
@@ -189,8 +206,9 @@
 
 
 class Weight:
-    def __init__(self, at, factor, part, z_in, send, recv):
-        self.at, self.factor, self.part, self.z_in = at, factor, part, z_in
+    def __init__(self, at, line, cross, factor, part, arrived, send, recv):
+        self.at, self.line, self.cross = at, line, cross
+        self.factor, self.part, self.arrived = factor, part, arrived
         self.send, self.recv = send, recv
         self.sent = []
 
@@ -203,49 +221,49 @@
         copy_to(ref, ref, self.send.at[index], self.recv.at[index], self.at.other_core).wait_recv()
 
     def gather(self):
-        at = self.at
-        mine = self.factor.at[at.x]
-        self.go(mine, mine, 0, at.x_dev(at.xa))
-        self.go(mine, mine, 1, at.x_dev(at.xb))
+        line = self.line
+        mine = self.factor.at[line.me]
+        self.go(mine, mine, 0, line.device(line.a))
+        self.go(mine, mine, 1, line.device(line.b))
 
     def gather_again(self):
-        at = self.at
-        theirs = self.factor.at[at.xa]
+        line = self.line
+        theirs = self.factor.at[line.a]
         self.wait(theirs, 0)
-        self.go(theirs, theirs, 2, at.x_dev(at.xb))
+        self.go(theirs, theirs, 2, line.device(line.b))
 
     def gathered(self):
-        at = self.at
-        self.wait(self.factor.at[at.xb], 1)
-        self.wait(self.factor.at[at.x2], 2)
-
-    def block(self, z, own, spread):
-        at = self.at
-        total = dot_nn(self.factor[at.x], own[:, rows_of(at.x * 1024 + z * 256, 256)])
+        line = self.line
+        self.wait(self.factor.at[line.b], 1)
+        self.wait(self.factor.at[line.far], 2)
+
+    def block(self, j, own, spread):
+        line = self.line
+        total = dot_nn(self.factor[line.me], own[:, rows_of(line.column(line.me, j), 256)])
         for place in range(3):
-            peer = lax.rem(at.x + 1 + place, 4)
-            total += dot_nn(self.factor[peer], spread[place, :, rows_of(z * 256, 256)])
-        self.part[z] = total.astype(BF16)
+            peer = lax.rem(line.me + 1 + place, 4)
+            total += dot_nn(self.factor[peer], spread[place, :, rows_of(j * 256, 256)])
+        self.part[j] = total.astype(BF16)
 
     def product(self, own, spread):
-        at = self.at
-        self.block(at.z2, own, spread)
-        self.go(self.part.at[at.z2], self.z_in.at[0], 3, at.z_dev(at.za))
-        self.block(at.za, own, spread)
-        self.go(self.part.at[at.za], self.z_in.at[1], 4, at.z_dev(at.za))
-        self.block(at.zb, own, spread)
-        self.block(at.z, own, spread)
+        cross = self.cross
+        self.block(cross.far, own, spread)
+        self.go(self.part.at[cross.far], self.arrived.at[0], 3, cross.device(cross.a))
+        self.block(cross.a, own, spread)
+        self.go(self.part.at[cross.a], self.arrived.at[1], 4, cross.device(cross.a))
+        self.block(cross.b, own, spread)
+        self.block(cross.me, own, spread)
 
     def second(self):
-        at = self.at
-        self.wait(self.z_in.at[0], 3)
-        self.part[at.zb] = (self.part[at.zb].astype(F32) + self.z_in[0].astype(F32)).astype(BF16)
-        self.go(self.part.at[at.zb], self.z_in.at[2], 5, at.z_dev(at.zb))
+        cross = self.cross
+        self.wait(self.arrived.at[0], 3)
+        self.part[cross.b] = (self.part[cross.b].astype(F32) + self.arrived[0].astype(F32)).astype(BF16)
+        self.go(self.part.at[cross.b], self.arrived.at[2], 5, cross.device(cross.b))
 
     def total(self):
-        self.wait(self.z_in.at[1], 4)
-        self.wait(self.z_in.at[2], 5)
-        return self.part[self.at.z].astype(F32) + self.z_in[1].astype(F32) + self.z_in[2].astype(F32)
+        self.wait(self.arrived.at[1], 4)
+        self.wait(self.arrived.at[2], 5)
+        return self.part[self.cross.me].astype(F32) + self.arrived[1].astype(F32) + self.arrived[2].astype(F32)
 
 
 class Place:
@@ -254,19 +272,13 @@
         self.mp = lax.axis_index("mp")
         self.x, self.z = lax.div(self.dp, 4), lax.rem(self.dp, 4)
         self.y, self.c = lax.div(self.mp, 2), lax.rem(self.mp, 2)
-        self.xa, self.xb, self.x2 = partners(self.x, self.c)
         self.ya, self.yb, self.y2 = partners(self.y, self.c)
-        self.za, self.zb, self.z2 = partners(self.z, self.c)
         self.other_core = (self.dp, self.y * 2 + 1 - self.c)
-
-    def x_dev(self, x):
-        return (x * 4 + self.z, self.mp)
+        self.along_x = Line(self.x, self.c, lambda x: (x * 4 + self.z, self.mp), 1024, 256)
+        self.along_z = Line(self.z, self.c, lambda z: (self.x * 4 + z, self.mp), 256, 1024)
 
     def y_dev(self, y):
         return (self.dp, y * 2 + self.c)
-
-    def z_dev(self, z):
-        return (self.x * 4 + z, self.mp)
 
 
 def head(h):
@@ -287,27 +299,52 @@
     return factor[h][:, :1] * (upstream - rows * mean)
 
 
+def placements(at, enc_len, dec_len, perm, offset, pack, unpack, mask):
+    row = lax.broadcasted_iota(jnp.int32, (1, ENC), 1)
+    target = jnp.zeros((1, ENC), jnp.int32)
+    start = 0
+    for k in range(SLOTS):
+        owner = perm[lax.rem(at.dp + offset[k], SLOTS)]
+        end = start + enc_len[at.dp, k]
+        target = jnp.where((row >= start) & (row < end), owner * CAP + row - start, target)
+        start = end
+    chosen = lax.broadcasted_iota(jnp.int32, (SLOTS * CAP, ENC), 0) == target
+    chosen = jnp.where(chosen, 1.0, 0.0).astype(F32)
+    pack[...] = chosen.astype(BF16)
+    unpack[...] = chosen.T.astype(BF16)
+
+    here = 0
+    for p in range(SLOTS):
+        here = jnp.where(perm[p] == at.dp, p, here)
+    arrived = lax.broadcasted_iota(jnp.int32, (1, SLOTS * CAP), 1)
+    key_slot = jnp.full((1, SLOTS * CAP), -1, jnp.int32)
+    row = lax.broadcasted_iota(jnp.int32, (DEC, 128), 0)
+    slot = jnp.zeros((DEC, 128), jnp.int32)
+    end = 0
+    for k in range(SLOTS):
+        source = lax.rem(here - offset[k] + SLOTS, SLOTS)
+        first = source * CAP
+        key_slot = jnp.where((arrived >= first) & (arrived < first + enc_len[source, k]), k, key_slot)
+        end = end + dec_len[at.dp, k]
+        slot = jnp.where(row >= end, k + 1, slot)
+    for half in range(2):
+        cols = slice(half * 128, (half + 1) * 128)
+        mask[:, cols] = jnp.where(slot == key_slot[:, cols], 1.0, 0.0).astype(F32)
+
+
 def kernel(
-    enc_h, dec_h, go_h, wq_h, wk_h, wv_h, wo_h, pack_ref, unpack_ref, mask_ref,
+    enc_h, dec_h, go_h, wq_h, wk_h, wv_h, wo_h, enc_len, dec_len, perm, offset,
     mixed_h, decg_h, encg_h, gq_h, gk_h, gv_h, gp_h,
     enc, dec, go, wq, wk, wv, wo,
     xdec, xgo, xenc,
-    raw_d, raw_e, qu, qa, ku, kb, r_dec, qb, up, kv, kv_out, kv_in, g_out, g_in, probs, att, dqb, dkb, dvb,
+    pack_ref, unpack_ref, mask_ref,
+    raw_d, raw_e, qu, qa, ku, kb, r_dec, qb, up, k_out, v_out, k_in, v_in, g_out, g_in, probs, att, dqb, dkb, dvb,
     p_mix, c_mix, y_mix, f_mix, p_dec, c_dec, y_dec, f_dec, p_enc, c_enc, y_enc, f_enc,
     fq, fk, fv, fp, pq, pk, pv, pp, zq, zk, zv, zp, oq, ok, ov, op,
-    load_sem, kv_send, kv_recv, g_send, g_recv, x_send, x_recv, s_send, s_recv, s_local, w_send, w_recv, w_local,
+    load_sem, k_send, k_recv, v_send, v_recv, g_send, g_recv, x_send, x_recv, s_send, s_recv, s_local,
+    w_send, w_recv, w_local,
 ):
     at = Place()
-
-    loads = []
-    for src, dst in (
-        (enc_h, enc), (wk_h, wk), (wv_h, wv), (dec_h, dec), (wq_h, wq), (go_h, go), (wo_h, wo),
-    ):
-        copy = pltpu.make_async_copy(src, dst, load_sem.at[len(loads)])
-        copy.start()
-        loads.append(copy)
-    l_enc, l_wk, l_wv, l_dec, l_wq, l_go, l_wo = loads
-
     barrier = pltpu.get_barrier_semaphore()
 
     @pl.loop(1, 16)
@@ -318,14 +355,24 @@
 
     for device in (at.other_core, at.y_dev(at.ya), at.y_dev(at.yb)):
         pl.semaphore_signal(barrier, inc=1, device_id=device, device_id_type=MESH)
+
+    def load(number, src, dst):
+        copy = pltpu.make_async_copy(src, dst, load_sem.at[number])
+        copy.start()
+        return copy
+
+    l_enc = load(0, enc_h, enc)
+    l_wk = load(1, wk_h, wk)
+    l_wv = load(2, wv_h, wv)
+    placements(at, enc_len, dec_len, perm, offset, pack_ref, unpack_ref, mask_ref)
     pl.semaphore_wait(barrier, 18)
 
-    s_dec = Spread(at, dec_h, xdec, x_send.at[0], x_recv.at[0])
-    s_go = Spread(at, go_h, xgo, x_send.at[1], x_recv.at[1])
-    s_enc = Spread(at, enc_h, xenc, x_send.at[2], x_recv.at[2])
+    s_dec = Spread(at, at.along_z, dec_h, xdec, x_send.at[0], x_recv.at[0])
+    s_go = Spread(at, at.along_x, go_h, xgo, x_send.at[1], x_recv.at[1])
+    s_enc = Spread(at, at.along_x, enc_h, xenc, x_send.at[2], x_recv.at[2])
     spreads = (s_go, s_dec, s_enc)
     for spread in spreads:
-        spread.over_x()
+        spread.over_line()
 
     def project(total, rows, weight):
         total[...] = jnp.zeros_like(total)
@@ -334,18 +381,6 @@
         def _(k):
             cols = rows_of(k * 1024, 1024)
             total[...] += dot_nn(rows[:, cols], weight[cols, :])
-
-    l_enc.wait()
-    l_wk.wait()
-    project(raw_e, enc, wk)
-    unit_heads(raw_e, ku, kb)
-    kv[:, :COLS] = ku[...].astype(BF16)
-    l_wv.wait()
-    project(raw_e, enc, wv)
-    kv[:, COLS:] = raw_e[...].astype(BF16)
-    for half in range(2):
-        cols = slice(half * COLS, (half + 1) * COLS)
-        kv_out[:, cols] = dot_nn(pack_ref[...], kv[:, cols]).astype(BF16)
 
     def exchange(source, target, send, recv):
         @pl.loop(1, 16)
@@ -369,10 +404,21 @@
             block = rows_of(peer * CAP, CAP)
             copy_to(source.at[block], target.at[block], send.at[peer], recv.at[peer], (peer, at.mp)).wait()
 
-    exchange(kv_out, kv_in, kv_send, kv_recv)
-
-    for spread in spreads:
-        spread.over_y()
+    l_enc.wait()
+    l_wk.wait()
+    l_dec = load(3, dec_h, dec)
+    l_wq = load(4, wq_h, wq)
+    project(raw_e, enc, wk)
+    unit_heads(raw_e, ku, kb)
+    k_out[...] = dot_nn(pack_ref[...], ku[...].astype(BF16)).astype(BF16)
+    exchange(k_out, k_in, k_send, k_recv)
+    l_wv.wait()
+    l_go = load(5, go_h, go)
+    l_wo = load(6, wo_h, wo)
+    project(raw_e, enc, wv)
+    v_out[...] = dot_nn(pack_ref[...], raw_e[...].astype(BF16)).astype(BF16)
+    exchange(v_out, v_in, v_send, v_recv)
+
     l_dec.wait()
     raw_d[...] = jnp.zeros_like(raw_d)
 
@@ -385,6 +431,8 @@
         lax.rsqrt(jnp.sum(raw_d[...], axis=1, keepdims=True) * (1.0 / D) + EPS), r_dec.shape
     )
     l_wq.wait()
+    for spread in spreads:
+        spread.over_y()
     raw_d[...] = jnp.zeros_like(raw_d)
 
     @pl.loop(0, 4)
@@ -396,8 +444,6 @@
     unit_heads(raw_d, qu, qa)
     qb[...] = qu[...].astype(BF16)
 
-    for spread in spreads:
-        spread.over_y_again()
     l_go.wait()
     l_wo.wait()
     raw_d[...] = jnp.zeros_like(raw_d)
@@ -408,20 +454,22 @@
         raw_d[...] += dot_nt(go[:, cols], wo[:, cols])
 
     up[...] = raw_d[...].astype(BF16)
-    for spread in spreads:
-        spread.over_core()
-
-    grad_q = Weight(at, fq, pq, zq, w_send.at[0], w_recv.at[0])
-    grad_k = Weight(at, fk, pk, zk, w_send.at[1], w_recv.at[1])
-    grad_v = Weight(at, fv, pv, zv, w_send.at[2], w_recv.at[2])
-    grad_p = Weight(at, fp, pp, zp, w_send.at[3], w_recv.at[3])
+
+    def weight(number, line, cross, factor, part, arrived):
+        return Weight(at, line, cross, factor, part, arrived, w_send.at[number], w_recv.at[number])
+
+    grad_q = weight(0, at.along_z, at.along_x, fq, pq, zq)
+    grad_k = weight(1, at.along_x, at.along_z, fk, pk, zk)
+    grad_v = weight(2, at.along_x, at.along_z, fv, pv, zv)
+    grad_p = weight(3, at.along_x, at.along_z, fp, pp, zp)
     s_mix = Summed(at, p_mix, c_mix, y_mix, f_mix, mixed_h, s_send.at[0], s_recv.at[0], s_local.at[0])
     s_dng = Summed(at, p_dec, c_dec, y_dec, f_dec, decg_h, s_send.at[1], s_recv.at[1], s_local.at[1])
     s_eng = Summed(at, p_enc, c_enc, y_enc, f_enc, encg_h, s_send.at[2], s_recv.at[2], s_local.at[2])
 
-    exchanged(kv_out, kv_in, kv_send, kv_recv)
+    exchanged(k_out, k_in, k_send, k_recv)
+    exchanged(v_out, v_in, v_send, v_recv)
     for h in range(2):
-        keys, values = kv_in[:, head(h)], kv_in[:, head(h + 2)]
+        keys, values = k_in[:, head(h)], v_in[:, head(h)]
         scores = dot_nt(qb[:, head(h)], keys) * SCALE
         weights = jnp.where(mask_ref[...] > 0.0, jnp.exp(scores), 0.0).astype(BF16)
         wide = weights.astype(F32)
@@ -446,7 +494,7 @@
     mix(at.c)
 
     for h in range(2):
-        keys, values = kv_in[:, head(h)], kv_in[:, head(h + 2)]
+        keys, values = k_in[:, head(h)], v_in[:, head(h)]
         upstream = up[:, head(h)]
         weighting = probs[h]
         delta = jnp.sum(upstream.astype(F32) * raw_d[:, head(h)], axis=1, keepdims=True)
@@ -456,7 +504,7 @@
         dquery = dot_nn(dscore.astype(BF16), keys)
         dq_raw = head_back(dquery, qu, qa, h)
         dqb[:, head(h)] = dq_raw.astype(BF16)
-        fq[at.x, head(h), :] = (dq_raw * r_dec[:, :1]).T.astype(BF16)
+        fq[at.z, head(h), :] = (dq_raw * r_dec[:, :1]).T.astype(BF16)
     exchange(g_out, g_in, g_send, g_recv)
     grad_q.gather()
     s_mix.first()
@@ -472,8 +520,10 @@
     dnormed(1 - at.c)
     s_dng.over_core()
     dnormed(at.c)
+    for spread in spreads:
+        spread.over_y_again()
     grad_p.gather_again()
-    s_mix.second()
+    s_dng.first()
 
     exchanged(g_out, g_in, g_send, g_recv)
     for h in range(2):
@@ -486,8 +536,6 @@
         fv[at.x, head(h), :] = dvalue.T.astype(BF16)
     grad_k.gather()
     grad_v.gather()
-    grad_q.gather_again()
-    s_dng.first()
 
     @pl.loop(0, 4)
     def _(k):
@@ -495,25 +543,32 @@
         p_enc[:, cols] = (dot_nt(dkb[...], wk[cols, :]) + dot_nt(dvb[...], wv[cols, :])).astype(BF16)
 
     s_eng.over_core()
+    for spread in spreads:
+        spread.over_core()
+    grad_q.gather_again()
+    s_mix.second()
+
+    s_go.finish()
+    grad_p.gathered()
+    grad_p.product(go, xgo)
+    s_eng.first()
+    s_dng.second()
+    grad_k.gather_again()
+    grad_v.gather_again()
+
+    s_dec.finish()
+    grad_q.gathered()
+    grad_q.product(dec, xdec)
 
     mine_d = rows_of((at.c * 4 + at.y) * 32, 32)
     f_mix[...] = (dec[mine_d, :].astype(F32) + s_mix.total()).astype(BF16)
     s_mix.share()
-
-    s_go.finish()
-    grad_p.gathered()
-    grad_p.product(go, xgo)
-    s_dng.second()
-    s_eng.first()
-    grad_k.gather_again()
-    grad_v.gather_again()
-    s_mix.forward()
-
-    s_dec.finish()
-    grad_q.gathered()
-    grad_q.product(dec, xdec)
+    grad_p.second()
     s_eng.second()
-    grad_p.second()
+
+    s_enc.finish()
+    grad_k.gathered()
+    grad_k.product(enc, xenc)
 
     total = s_dng.total()
     unit = dec[mine_d, :].astype(F32) * r_dec[mine_d, :1]
@@ -521,17 +576,13 @@
     back = r_dec[mine_d, :1] * (total - unit * mean)
     f_dec[...] = (go[mine_d, :].astype(F32) + back).astype(BF16)
     s_dng.share()
-    s_mix.forward_last()
-
-    s_enc.finish()
-    grad_k.gathered()
-    grad_k.product(enc, xenc)
+
+    grad_q.second()
     grad_v.gathered()
     grad_v.product(enc, xenc)
+    s_mix.forward()
     f_enc[...] = s_eng.total().astype(BF16)
     s_eng.share()
-    grad_q.second()
-    s_dng.forward()
 
     outs = []
 
@@ -543,11 +594,13 @@
     op[...] = grad_p.total()
     store(op, gp_h)
     grad_k.second()
+    s_dng.forward()
+    s_mix.forward_last()
     grad_v.second()
+    oq[...] = grad_q.total().T
+    store(oq, gq_h)
     s_eng.forward()
     s_dng.forward_last()
-    oq[...] = grad_q.total().T
-    store(oq, gq_h)
     ok[...] = grad_k.total().T
     store(ok, gk_h)
     ov[...] = grad_v.total().T
@@ -562,49 +615,21 @@
             copy.wait_send()
 
 
-def tables(enc_len, dec_len, device_perm, slot_offset):
-    here = lax.axis_index("dp")
-    slots = jnp.arange(SLOTS, dtype=jnp.int32)
-    owners = jnp.take(device_perm, (slots[:, None] + slot_offset[None, :]) % SLOTS, axis=0)
-
-    def placed(lengths, rows):
-        ends = jnp.cumsum(lax.dynamic_index_in_dim(lengths, here, 0, False), dtype=jnp.int32)
-        past = jnp.arange(rows, dtype=jnp.int32)[:, None] >= ends[None, :]
-        slot = jnp.sum(past.astype(jnp.int32), axis=1)
-        return slot, jnp.max(jnp.where(past, ends[None, :], 0), axis=1)
-
-    slot, start = placed(enc_len, ENC)
-    mine = lax.dynamic_index_in_dim(owners, here, 0, False)
-    owner = jnp.sum(jnp.where(slot[:, None] == slots[None, :], mine[None, :], 0), axis=1)
-    target = owner * CAP + jnp.arange(ENC, dtype=jnp.int32) - start
-    pack = jnp.arange(SLOTS * CAP, dtype=jnp.int32)[:, None] == target[None, :]
-    unpack = target[:, None] == jnp.arange(SLOTS * CAP, dtype=jnp.int32)[None, :]
-
-    chosen = owners == here
-    key_slot = jnp.sum(jnp.where(chosen, slots[None, :], 0), axis=1)
-    key_len = jnp.sum(jnp.where(chosen, enc_len, 0), axis=1)
-    key_id = jnp.where(slots[None, :] < key_len[:, None], key_slot[:, None], -1).reshape(-1)
-    dec_slot, _ = placed(dec_len, DEC)
-    mask = dec_slot[:, None] == key_id[None, :]
-    return pack.astype(BF16), unpack.astype(BF16), mask.astype(F32)
-
-
 def body(enc, dec, grad_out, w_query, w_key, w_value, w_out, enc_len, dec_len, device_perm, slot_offset):
-    pack, unpack, mask = tables(enc_len, dec_len, device_perm, slot_offset)
     anywhere = pl.BlockSpec(memory_space=pl.ANY)
-    whole = pl.BlockSpec(memory_space=pltpu.VMEM)
+    scalars = pl.BlockSpec(memory_space=pltpu.SMEM)
     vmem = pltpu.VMEM
     dma = pltpu.SemaphoreType.DMA
     scratch = [
         vmem((ENC, D), BF16), vmem((DEC, D), BF16), vmem((DEC, D), BF16),
         vmem((D, COLS), BF16), vmem((D, COLS), BF16), vmem((D, COLS), BF16), vmem((COLS, D), BF16),
         vmem((3, DEC, 1024), BF16), vmem((3, DEC, 1024), BF16), vmem((3, ENC, 1024), BF16),
+        vmem((256, ENC), BF16), vmem((ENC, 256), BF16), vmem((DEC, 256), F32),
         vmem((DEC, COLS), F32), vmem((ENC, COLS), F32),
         vmem((DEC, COLS), F32), vmem((2, DEC, 128), F32),
         vmem((ENC, COLS), F32), vmem((2, ENC, 128), F32),
         vmem((DEC, 128), F32), vmem((DEC, COLS), BF16), vmem((DEC, COLS), BF16),
-        vmem((ENC, 2 * COLS), BF16),
-        vmem((256, 2 * COLS), BF16), vmem((256, 2 * COLS), BF16),
+        vmem((256, COLS), BF16), vmem((256, COLS), BF16), vmem((256, COLS), BF16), vmem((256, COLS), BF16),
         vmem((256, 2 * COLS), BF16), vmem((256, 2 * COLS), BF16),
         vmem((2, DEC, 256), F32), vmem((DEC, COLS), BF16), vmem((DEC, COLS), BF16),
         vmem((ENC, COLS), BF16), vmem((ENC, COLS), BF16),
@@ -619,8 +644,8 @@
     scratch += [vmem((3, COLS, 256), BF16)] * 4
     scratch += [vmem((256, COLS), F32)] * 3 + [vmem((COLS, 256), F32)]
     scratch += [
-        dma((7,)), dma((16,)), dma((16,)), dma((16,)), dma((16,)),
-        dma((3, 7)), dma((3, 7)), dma((3, 11)), dma((3, 11)), dma((3,)),
+        dma((7,)), dma((16,)), dma((16,)), dma((16,)), dma((16,)), dma((16,)), dma((16,)),
+        dma((3, 19)), dma((3, 19)), dma((3, 11)), dma((3, 11)), dma((3,)),
         dma((4, 6)), dma((4, 6)), dma((4,)),
     ]
     return pl.pallas_call(
@@ -634,14 +659,14 @@
             jax.ShapeDtypeStruct((256, COLS), F32),
             jax.ShapeDtypeStruct((COLS, 256), F32),
         ),
-        in_specs=[anywhere] * 7 + [whole] * 3,
+        in_specs=[anywhere] * 7 + [scalars] * 4,
         out_specs=[anywhere] * 7,
         scratch_shapes=scratch,
         compiler_params=pltpu.CompilerParams(
             collective_id=0, has_side_effects=True, vmem_limit_bytes=60 * 1024 * 1024
         ),
         name="cross_attention",
-    )(enc, dec, grad_out, w_query, w_key, w_value, w_out, pack, unpack, mask)
+    )(enc, dec, grad_out, w_query, w_key, w_value, w_out, enc_len, dec_len, device_perm, slot_offset)
 
 
 def solution(mesh):

time: 123 us -> 94.8 us (0.77)
  Pallas kernels: 104 us -> 82.7 us
  other arithmetic: 3.64 us -> 0 us
  local copies, waits for them, and re-layouts: 12.8 us -> 9.79 us
    pallas_call x1, Pallas kernels: 104 us -> 82.7 us  [body(): pl.pallas_call(kernel, out_shape=(jax.ShapeDtypeStruct((DEC, D), BF16), j...]
    convert_element_type x3 -> x0, other arithmetic: 2.17 us -> none  [tables(): return (pack.astype(BF16), unpack.astype(BF16), mask.astype(F32))]
    gather x2 -> x0, local copies, waits for them, and re-layouts: 1.94 us -> none  [tables(): jnp.take(device_perm, (slots[:, None] + slot_offset[None, :]) % SLOTS, ax...]
    unnamed x25 -> x19, local copies, waits for them, and re-layouts: 9.81 us -> 9.79 us
where the time goes in v2:
time: 94.8 us; the launch traced here: 93.1 us
  Pallas kernels  82.7 us (87%)
  local copies, waits for them, and re-layouts  9.79 us (10%)
    pallas_call x1, Pallas kernels, body(): pl.pallas_call(kernel, out_shape=(jax.ShapeDtypeStruct((DEC, D), BF16), j...  82.7 us
    unnamed x19, local copies, waits for them, and re-layouts  9.79 us

profile of v2, /device:TPU:0, one launch (start us, length us, event | category | flops | bytes accessed | tf_op | source)
XLA Modules:
  0.0 93.1 jit_solution(11360619615709757308)
XLA Ops:
  0.6 82.7 %cross_attention.1 = (bf16[256,4096]{1,0:T(8,128)(2,1)}, bf16[256,4096]{1,0:T(8,128)(2,1)}, bf16[128,4096]{1,0:T(8,128)(2,1)}, f32[256,512]{1,0:T(8,128)}, f32[2...) custom-call(bf16[128,4096]{1,0:T(8,128)(2,1)} %enc_h.1, bf16[256,4096]{1,0:T(8,128)(2,1)} %dec_h.1, ...), custom_call_target="tpu_custom_call" | custom-call | tf_op jit(solution)/shard_map/cross_attention/pallas_call | solution.py:651
  83.3 0.0 copy-start
  83.3 3.3 %copy.25 = bf16[256,4096]{1,0:T(8,128)(2,1)} copy(bf16[256,4096]{1,0:T(8,128)(2,1)} %get-tuple-element.14) | data formatting | bytes 4194304
  86.6 0.0 copy-done
  86.6 0.0 copy-start.1
  86.6 1.3 %copy.26 = bf16[256,4096]{1,0:T(8,128)(2,1)} copy(bf16[256,4096]{1,0:T(8,128)(2,1)S(1)} %copy-done) | data formatting | bytes 4194304
  87.9 0.6 copy-done.1
  88.6 0.0 copy-start.5
  88.6 0.0 copy-start.4
  88.6 0.0 copy-start.3
  88.6 1.0 %copy.27 = bf16[128,4096]{1,0:T(8,128)(2,1)} copy(bf16[128,4096]{1,0:T(8,128)(2,1)S(1)} %copy-done.1) | data formatting | bytes 2097152
  89.6 0.4 copy-done.5
  90.0 0.0 copy-start.2
  90.0 0.8 copy.28
  90.7 0.0 copy-done.4
  90.8 0.8 copy.29
  91.5 0.0 copy-done.3
  91.5 0.8 copy.30
  92.3 0.0 copy-done.2
  92.3 0.8 copy.31
Async XLA Ops:
  83.3 3.3 %copy-start = (bf16[256,4096]{1,0:T(8,128)(2,1)S(1)}, bf16[256,4096]{1,0:T(8,128)(2,1)}, u32[]{:S(2)}) copy-start(bf16[256,4096]{1,0:T(8,128)(2,1)} %get-tuple-element.15) | copy-start | bytes 6291460
  86.6 2.0 %copy-start.1 = (bf16[128,4096]{1,0:T(8,128)(2,1)S(1)}, bf16[128,4096]{1,0:T(8,128)(2,1)}, u32[]{:S(2)}) copy-start(bf16[128,4096]{1,0:T(8,128)(2,1)} %get-tuple-element.16) | copy-start | bytes 3145732
  88.6 1.4 %copy-start.5 = (f32[256,512]{1,0:T(8,128)S(1)}, f32[256,512]{1,0:T(8,128)}, u32[]{:S(2)}) copy-start(f32[256,512]{1,0:T(8,128)} %get-tuple-element.17) | copy-start | bytes 1572868
  88.6 2.2 %copy-start.4 = (f32[256,512]{1,0:T(8,128)S(1)}, f32[256,512]{1,0:T(8,128)}, u32[]{:S(2)}) copy-start(f32[256,512]{1,0:T(8,128)} %get-tuple-element.18) | copy-start | bytes 1572868
  88.6 3.0 %copy-start.3 = (f32[256,512]{1,0:T(8,128)S(1)}, f32[256,512]{1,0:T(8,128)}, u32[]{:S(2)}) copy-start(f32[256,512]{1,0:T(8,128)} %get-tuple-element.19) | copy-start | bytes 1572868
  90.0 2.4 %copy-start.2 = (f32[512,256]{1,0:T(8,128)S(1)}, f32[512,256]{1,0:T(8,128)}, u32[]{:S(2)}) copy-start(f32[512,256]{1,0:T(8,128)} %get-tuple-element.20) | copy-start | bytes 1572868

commit v3 on v2

--- a/solution.py
+++ b/solution.py
@@ -123,9 +123,9 @@
 
 
 class Summed:
-    def __init__(self, at, part, core_in, y_in, final, out, send, recv, local):
+    def __init__(self, at, part, core_in, y_in, out, send, recv):
         self.at, self.part, self.core_in, self.y_in = at, part, core_in, y_in
-        self.final, self.out, self.send, self.recv, self.local = final, out, send, recv, local
+        self.out, self.send, self.recv = out, send, recv
         self.half = part.shape[0] // 2
         self.rows = part.shape[0] // 8
         self.sent = []
@@ -174,13 +174,13 @@
         rows = self.rows_at(self.at.y)
         return self.part[rows, :].astype(F32) + self.y_in[1].astype(F32) + self.y_in[2].astype(F32)
 
-    def share(self):
-        at = self.at
-        rows = self.rows_at(at.y)
-        self.go(self.final, self.out.at[rows], 4, at.y_dev(at.ya))
-        self.go(self.final, self.out.at[rows], 5, at.y_dev(at.yb))
-        self.go(self.final, self.out.at[rows], 7, at.other_core)
-        pltpu.make_async_copy(self.final, self.out.at[rows], self.local).start()
+    def share(self, final):
+        at = self.at
+        self.out[self.rows_at(at.y), :] = final.astype(BF16)
+        rows = self.out.at[self.rows_at(at.y)]
+        self.go(rows, rows, 4, at.y_dev(at.ya))
+        self.go(rows, rows, 5, at.y_dev(at.yb))
+        self.go(rows, rows, 7, at.other_core)
 
     def forward(self):
         at = self.at
@@ -202,7 +202,6 @@
         other = 1 - at.c
         for index, y in ((7, at.y), (8, at.yb), (9, at.ya), (10, at.y2)):
             self.wait(self.out.at[self.rows_at(y, other)], index)
-        pltpu.make_async_copy(self.final, self.out.at[self.rows_at(at.y)], self.local).wait()
 
 
 class Weight:
@@ -334,15 +333,15 @@
 
 def kernel(
     enc_h, dec_h, go_h, wq_h, wk_h, wv_h, wo_h, enc_len, dec_len, perm, offset,
-    mixed_h, decg_h, encg_h, gq_h, gk_h, gv_h, gp_h,
+    mixed, decg, encg, gq, gk, gv, gp,
     enc, dec, go, wq, wk, wv, wo,
     xdec, xgo, xenc,
     pack_ref, unpack_ref, mask_ref,
     raw_d, raw_e, qu, qa, ku, kb, r_dec, qb, up, k_out, v_out, k_in, v_in, g_out, g_in, probs, att, dqb, dkb, dvb,
-    p_mix, c_mix, y_mix, f_mix, p_dec, c_dec, y_dec, f_dec, p_enc, c_enc, y_enc, f_enc,
-    fq, fk, fv, fp, pq, pk, pv, pp, zq, zk, zv, zp, oq, ok, ov, op,
-    load_sem, k_send, k_recv, v_send, v_recv, g_send, g_recv, x_send, x_recv, s_send, s_recv, s_local,
-    w_send, w_recv, w_local,
+    p_mix, c_mix, y_mix, p_dec, c_dec, y_dec, p_enc, c_enc, y_enc,
+    fq, fk, fv, fp, pq, pk, pv, pp, zq, zk, zv, zp,
+    load_sem, k_send, k_recv, v_send, v_recv, g_send, g_recv, x_send, x_recv, s_send, s_recv,
+    w_send, w_recv,
 ):
     at = Place()
     barrier = pltpu.get_barrier_semaphore()
@@ -462,9 +461,9 @@
     grad_k = weight(1, at.along_x, at.along_z, fk, pk, zk)
     grad_v = weight(2, at.along_x, at.along_z, fv, pv, zv)
     grad_p = weight(3, at.along_x, at.along_z, fp, pp, zp)
-    s_mix = Summed(at, p_mix, c_mix, y_mix, f_mix, mixed_h, s_send.at[0], s_recv.at[0], s_local.at[0])
-    s_dng = Summed(at, p_dec, c_dec, y_dec, f_dec, decg_h, s_send.at[1], s_recv.at[1], s_local.at[1])
-    s_eng = Summed(at, p_enc, c_enc, y_enc, f_enc, encg_h, s_send.at[2], s_recv.at[2], s_local.at[2])
+    s_mix = Summed(at, p_mix, c_mix, y_mix, mixed, s_send.at[0], s_recv.at[0])
+    s_dng = Summed(at, p_dec, c_dec, y_dec, decg, s_send.at[1], s_recv.at[1])
+    s_eng = Summed(at, p_enc, c_enc, y_enc, encg, s_send.at[2], s_recv.at[2])
 
     exchanged(k_out, k_in, k_send, k_recv)
     exchanged(v_out, v_in, v_send, v_recv)
@@ -561,8 +560,7 @@
     grad_q.product(dec, xdec)
 
     mine_d = rows_of((at.c * 4 + at.y) * 32, 32)
-    f_mix[...] = (dec[mine_d, :].astype(F32) + s_mix.total()).astype(BF16)
-    s_mix.share()
+    s_mix.share(dec[mine_d, :].astype(F32) + s_mix.total())
     grad_p.second()
     s_eng.second()
 
@@ -574,42 +572,27 @@
     unit = dec[mine_d, :].astype(F32) * r_dec[mine_d, :1]
     mean = jnp.mean(total * unit, axis=1, keepdims=True)
     back = r_dec[mine_d, :1] * (total - unit * mean)
-    f_dec[...] = (go[mine_d, :].astype(F32) + back).astype(BF16)
-    s_dng.share()
+    s_dng.share(go[mine_d, :].astype(F32) + back)
 
     grad_q.second()
     grad_v.gathered()
     grad_v.product(enc, xenc)
     s_mix.forward()
-    f_enc[...] = s_eng.total().astype(BF16)
-    s_eng.share()
-
-    outs = []
-
-    def store(source, target):
-        copy = pltpu.make_async_copy(source, target, w_local.at[len(outs)])
-        copy.start()
-        outs.append(copy)
-
-    op[...] = grad_p.total()
-    store(op, gp_h)
+    s_eng.share(s_eng.total())
+
+    gp[...] = grad_p.total()
     grad_k.second()
     s_dng.forward()
     s_mix.forward_last()
     grad_v.second()
-    oq[...] = grad_q.total().T
-    store(oq, gq_h)
+    gq[...] = grad_q.total().T
     s_eng.forward()
     s_dng.forward_last()
-    ok[...] = grad_k.total().T
-    store(ok, gk_h)
-    ov[...] = grad_v.total().T
-    store(ov, gv_h)
+    gk[...] = grad_k.total().T
+    gv[...] = grad_v.total().T
     s_eng.forward_last()
     for summed in (s_mix, s_dng, s_eng):
         summed.finish()
-    for copy in outs:
-        copy.wait()
     for user in (*spreads, s_mix, s_dng, s_eng, grad_q, grad_k, grad_v, grad_p):
         for copy in user.sent:
             copy.wait_send()
@@ -637,33 +620,27 @@
     for rows in (DEC, DEC, ENC):
         scratch += [
             vmem((rows, D), BF16), vmem((rows // 2, D), BF16),
-            vmem((3, rows // 8, D), BF16), vmem((rows // 8, D), BF16),
+            vmem((3, rows // 8, D), BF16),
         ]
     scratch += [vmem((4, COLS, rows), BF16) for rows in (DEC, ENC, ENC, DEC)]
     scratch += [vmem((4, COLS, 256), BF16)] * 4
     scratch += [vmem((3, COLS, 256), BF16)] * 4
-    scratch += [vmem((256, COLS), F32)] * 3 + [vmem((COLS, 256), F32)]
     scratch += [
         dma((7,)), dma((16,)), dma((16,)), dma((16,)), dma((16,)), dma((16,)), dma((16,)),
-        dma((3, 19)), dma((3, 19)), dma((3, 11)), dma((3, 11)), dma((3,)),
-        dma((4, 6)), dma((4, 6)), dma((4,)),
+        dma((3, 19)), dma((3, 19)), dma((3, 11)), dma((3, 11)),
+        dma((4, 6)), dma((4, 6)),
     ]
     return pl.pallas_call(
         kernel,
         out_shape=(
-            jax.ShapeDtypeStruct((DEC, D), BF16),
-            jax.ShapeDtypeStruct((DEC, D), BF16),
-            jax.ShapeDtypeStruct((ENC, D), BF16),
-            jax.ShapeDtypeStruct((256, COLS), F32),
-            jax.ShapeDtypeStruct((256, COLS), F32),
-            jax.ShapeDtypeStruct((256, COLS), F32),
-            jax.ShapeDtypeStruct((COLS, 256), F32),
+            vmem((DEC, D), BF16), vmem((DEC, D), BF16), vmem((ENC, D), BF16),
+            vmem((256, COLS), F32), vmem((256, COLS), F32), vmem((256, COLS), F32), vmem((COLS, 256), F32),
         ),
         in_specs=[anywhere] * 7 + [scalars] * 4,
-        out_specs=[anywhere] * 7,
+        out_specs=[pl.BlockSpec(memory_space=vmem)] * 7,
         scratch_shapes=scratch,
         compiler_params=pltpu.CompilerParams(
-            collective_id=0, has_side_effects=True, vmem_limit_bytes=60 * 1024 * 1024
+            collective_id=0, has_side_effects=True, vmem_limit_bytes=56 * 1024 * 1024
         ),
         name="cross_attention",
     )(enc, dec, grad_out, w_query, w_key, w_value, w_out, enc_len, dec_len, device_perm, slot_offset)

time: 94.8 us -> 91.1 us (0.961)
  local copies, waits for them, and re-layouts: 9.79 us -> 6.78 us
    unnamed x19 -> x7, local copies, waits for them, and re-layouts: 9.79 us -> 6.78 us
where the time goes in v3:
time: 91.1 us; the launch traced here: 89.6 us
  Pallas kernels  82.2 us (90%)
  local copies, waits for them, and re-layouts  6.78 us (7%)
    pallas_call x1, Pallas kernels, body(): pl.pallas_call(kernel, out_shape=(vmem((DEC, D), BF16), vmem((DEC, D), BF...  82.2 us
    unnamed x7, local copies, waits for them, and re-layouts  6.78 us

profile of v3, /device:TPU:0, one launch (start us, length us, event | category | flops | bytes accessed | tf_op | source)
XLA Modules:
  0.0 89.6 jit_solution(18190959231901568516)
XLA Ops:
  0.6 82.2 %cross_attention.1 = (bf16[256,4096]{1,0:T(8,128)(2,1)S(1)}, bf16[256,4096]{1,0:T(8,128)(2,1)S(1)}, bf16[128,4096]{1,0:T(8,128)(2,1)S(1)}, f32[256,512]{1,0:T(8,...) custom-call(bf16[128,4096]{1,0:T(8,128)(2,1)} %enc_h.1, ...), custom_call_target="tpu_custom_call" | custom-call | tf_op jit(solution)/shard_map/cross_attention/pallas_call | solution.py:633
  82.8 1.3 %copy.25 = bf16[256,4096]{1,0:T(8,128)(2,1)} copy(bf16[256,4096]{1,0:T(8,128)(2,1)S(1)} %get-tuple-element.7) | data formatting | bytes 4194304
  84.1 0.8 copy.28
  84.9 0.8 copy.29
  85.7 0.8 copy.30
  86.5 0.8 copy.31
  87.3 1.0 %copy.27 = bf16[128,4096]{1,0:T(8,128)(2,1)} copy(bf16[128,4096]{1,0:T(8,128)(2,1)S(1)} %get-tuple-element.9) | data formatting | bytes 2097152
  88.3 1.3 %copy.26 = bf16[256,4096]{1,0:T(8,128)(2,1)} copy(bf16[256,4096]{1,0:T(8,128)(2,1)S(1)} %get-tuple-element.8) | data formatting | bytes 4194304

commit v4 on v3

--- a/solution.py
+++ b/solution.py
@@ -60,13 +60,15 @@
 
 
 class Spread:
-    def __init__(self, at, line, source, target, send, recv):
+    def __init__(self, at, line, pairs, source, target, send, recv):
         self.at, self.line, self.source, self.target, self.send, self.recv = at, line, source, target, send, recv
-        self.rows = target.shape[1] // 8
+        self.half = target.shape[1] // 2
+        self.rows = self.half // pairs
+        odd = lax.rem(at.y, 2) if pairs == 2 else 0
+        self.mine = rows_of(at.c * self.half + odd * self.rows, self.rows)
+        self.theirs = rows_of(at.c * self.half + (1 - odd) * self.rows, self.rows)
+        self.pairs = pairs
         self.sent = []
-
-    def chunk(self, y):
-        return self.target.at[:, rows_of((self.at.c * 4 + y) * self.rows, self.rows), :]
 
     def go(self, src, dst, index, device):
         copy = copy_to(src, dst, self.send.at[index], self.recv.at[index], device)
@@ -82,44 +84,43 @@
         return [(7 + place * 4 + j, slice(j * 256, (j + 1) * 256), j) for j in range(4)]
 
     def over_line(self):
-        at, line = self.at, self.line
-        mine = rows_of((at.c * 4 + at.y) * self.rows, self.rows)
+        line = self.line
         for off in (1, 3, 2):
             peer = lax.rem(line.me + off, 4)
             for index, cols, j in self.blocks(3 - off):
                 width = cols.stop - cols.start
                 self.go(
-                    self.source.at[mine, rows_of(line.column(peer, j), width)],
-                    self.target.at[3 - off, mine, cols],
+                    self.source.at[self.mine, rows_of(line.column(peer, j), width)],
+                    self.target.at[3 - off, self.mine, cols],
                     index,
                     line.device(peer),
                 )
 
+    def arrived(self):
+        for place in range(3):
+            for index, cols, _ in self.blocks(place):
+                self.wait(self.target.at[place, self.mine, cols], index)
+
     def over_y(self):
         at = self.at
-        mine = rows_of((at.c * 4 + at.y) * self.rows, self.rows)
-        for place in range(3):
-            for index, cols, _ in self.blocks(place):
-                self.wait(self.target.at[place, mine, cols], index)
-        self.go(self.chunk(at.y), self.chunk(at.y), 3, at.y_dev(at.ya))
-        self.go(self.chunk(at.y), self.chunk(at.y), 4, at.y_dev(at.yb))
-
-    def over_y_again(self):
-        at = self.at
-        self.wait(self.chunk(at.ya), 3)
-        self.go(self.chunk(at.ya), self.chunk(at.ya), 5, at.y_dev(at.yb))
+        self.arrived()
+        part = self.target.at[:, self.mine, :]
+        self.go(part, part, 3, at.y_dev(at.ya))
 
     def over_core(self):
-        at = self.at
-        self.wait(self.chunk(at.yb), 4)
-        self.wait(self.chunk(at.y2), 5)
-        half = self.target.at[:, rows_of(at.c * 4 * self.rows, 4 * self.rows), :]
-        self.go(half, half, 6, at.other_core)
+        if self.pairs == 2:
+            self.wait(self.target.at[:, self.theirs, :], 3)
+        else:
+            self.arrived()
+        half = self.target.at[:, rows_of(self.at.c * self.half, self.half), :]
+        self.go(half, half, 6, self.at.other_core)
 
     def finish(self):
-        at = self.at
-        half = self.target.at[:, rows_of((1 - at.c) * 4 * self.rows, 4 * self.rows), :]
-        self.wait(half, 6)
+        self.wait(self.target.at[:, rows_of((1 - self.at.c) * self.half, self.half), :], 6)
+
+
+def quarter(piece):
+    return slice(piece * 1024, (piece + 1) * 1024)
 
 
 class Summed:
@@ -142,9 +143,10 @@
         core = self.at.c if core is None else core
         return rows_of((core * 4 + y) * self.rows, self.rows)
 
-    def over_core(self):
-        other = 1 - self.at.c
-        self.go(self.part.at[rows_of(other * self.half, self.half)], self.core_in, 0, self.at.other_core)
+    def over_core(self, piece):
+        theirs = rows_of((1 - self.at.c) * self.half, self.half)
+        cols = quarter(piece)
+        self.go(self.part.at[theirs, cols], self.core_in.at[:, cols], 11 + piece, self.at.other_core)
 
     def add_core(self, y):
         rows = self.rows_at(y)
@@ -153,7 +155,8 @@
 
     def first(self):
         at = self.at
-        self.wait(self.core_in, 0)
+        for piece in range(4):
+            self.wait(self.core_in.at[:, quarter(piece)], 11 + piece)
         self.add_core(at.y2)
         self.go(self.part.at[self.rows_at(at.y2)], self.y_in.at[0], 1, at.y_dev(at.ya))
         self.add_core(at.ya)
@@ -332,9 +335,10 @@
 
 
 def kernel(
-    enc_h, dec_h, go_h, wq_h, wk_h, wv_h, wo_h, enc_len, dec_len, perm, offset,
+    enc_h, dec_h, go_h, wq_h, wk_h, wv_h, wo_h, enc_len_h, dec_len_h, perm_h, offset_h,
     mixed, decg, encg, gq, gk, gv, gp,
     enc, dec, go, wq, wk, wv, wo,
+    enc_len, dec_len, perm, offset,
     xdec, xgo, xenc,
     pack_ref, unpack_ref, mask_ref,
     raw_d, raw_e, qu, qa, ku, kb, r_dec, qb, up, k_out, v_out, k_in, v_in, g_out, g_in, probs, att, dqb, dkb, dvb,
@@ -360,18 +364,23 @@
         copy.start()
         return copy
 
+    scalars = [
+        load(7, enc_len_h, enc_len), load(8, dec_len_h, dec_len), load(9, perm_h, perm), load(10, offset_h, offset)
+    ]
     l_enc = load(0, enc_h, enc)
     l_wk = load(1, wk_h, wk)
     l_wv = load(2, wv_h, wv)
+    for copy in scalars:
+        copy.wait()
     placements(at, enc_len, dec_len, perm, offset, pack_ref, unpack_ref, mask_ref)
     pl.semaphore_wait(barrier, 18)
 
-    s_dec = Spread(at, at.along_z, dec_h, xdec, x_send.at[0], x_recv.at[0])
-    s_go = Spread(at, at.along_x, go_h, xgo, x_send.at[1], x_recv.at[1])
-    s_enc = Spread(at, at.along_x, enc_h, xenc, x_send.at[2], x_recv.at[2])
+    s_dec = Spread(at, at.along_z, 2, dec_h, xdec, x_send.at[0], x_recv.at[0])
+    s_go = Spread(at, at.along_x, 2, go_h, xgo, x_send.at[1], x_recv.at[1])
+    s_enc = Spread(at, at.along_x, 1, enc_h, xenc, x_send.at[2], x_recv.at[2])
     spreads = (s_go, s_dec, s_enc)
-    for spread in spreads:
-        spread.over_line()
+    s_go.over_line()
+    s_dec.over_line()
 
     def project(total, rows, weight):
         total[...] = jnp.zeros_like(total)
@@ -430,8 +439,8 @@
         lax.rsqrt(jnp.sum(raw_d[...], axis=1, keepdims=True) * (1.0 / D) + EPS), r_dec.shape
     )
     l_wq.wait()
-    for spread in spreads:
-        spread.over_y()
+    s_go.over_y()
+    s_dec.over_y()
     raw_d[...] = jnp.zeros_like(raw_d)
 
     @pl.loop(0, 4)
@@ -480,17 +489,10 @@
         fp[at.x, head(h), :] = heads_out.T.astype(BF16)
     grad_p.gather()
 
-    def mix(half):
-        rows = rows_of(half * 128, 128)
-
-        @pl.loop(0, 4)
-        def _(k):
-            cols = rows_of(k * 1024, 1024)
-            p_mix[rows, cols] = dot_nn(att[rows, :], wo[:, cols]).astype(BF16)
-
-    mix(1 - at.c)
-    s_mix.over_core()
-    mix(at.c)
+    for piece in range(4):
+        cols = quarter(piece)
+        p_mix[:, cols] = dot_nn(att[...], wo[:, cols]).astype(BF16)
+        s_mix.over_core(piece)
 
     for h in range(2):
         keys, values = k_in[:, head(h)], v_in[:, head(h)]
@@ -508,21 +510,17 @@
     grad_q.gather()
     s_mix.first()
 
-    def dnormed(half):
-        rows = rows_of(half * 128, 128)
-
-        @pl.loop(0, 4)
-        def _(k):
-            cols = rows_of(k * 1024, 1024)
-            p_dec[rows, cols] = dot_nt(dqb[rows, :], wq[cols, :]).astype(BF16)
-
-    dnormed(1 - at.c)
-    s_dng.over_core()
-    dnormed(at.c)
-    for spread in spreads:
-        spread.over_y_again()
+    for piece in range(4):
+        cols = quarter(piece)
+        p_dec[:, cols] = dot_nt(dqb[...], wq[cols, :]).astype(BF16)
+        s_dng.over_core(piece)
+
     grad_p.gather_again()
     s_dng.first()
+    s_go.over_core()
+    s_dec.over_core()
+    s_mix.second()
+    grad_q.gather_again()
 
     exchanged(g_out, g_in, g_send, g_recv)
     for h in range(2):
@@ -535,62 +533,56 @@
         fv[at.x, head(h), :] = dvalue.T.astype(BF16)
     grad_k.gather()
     grad_v.gather()
-
-    @pl.loop(0, 4)
-    def _(k):
-        cols = rows_of(k * 1024, 1024)
+    s_enc.over_line()
+
+    for piece in range(4):
+        cols = quarter(piece)
         p_enc[:, cols] = (dot_nt(dkb[...], wk[cols, :]) + dot_nt(dvb[...], wv[cols, :])).astype(BF16)
-
-    s_eng.over_core()
-    for spread in spreads:
-        spread.over_core()
-    grad_q.gather_again()
-    s_mix.second()
+        s_eng.over_core(piece)
+
+    s_dng.second()
 
     s_go.finish()
     grad_p.gathered()
     grad_p.product(go, xgo)
     s_eng.first()
-    s_dng.second()
+    mine_d = rows_of((at.c * 4 + at.y) * 32, 32)
+    s_mix.share(dec[mine_d, :].astype(F32) + s_mix.total())
+
+    s_enc.over_core()
     grad_k.gather_again()
     grad_v.gather_again()
-
     s_dec.finish()
     grad_q.gathered()
     grad_q.product(dec, xdec)
-
-    mine_d = rows_of((at.c * 4 + at.y) * 32, 32)
-    s_mix.share(dec[mine_d, :].astype(F32) + s_mix.total())
-    grad_p.second()
     s_eng.second()
-
-    s_enc.finish()
-    grad_k.gathered()
-    grad_k.product(enc, xenc)
 
     total = s_dng.total()
     unit = dec[mine_d, :].astype(F32) * r_dec[mine_d, :1]
     mean = jnp.mean(total * unit, axis=1, keepdims=True)
     back = r_dec[mine_d, :1] * (total - unit * mean)
     s_dng.share(go[mine_d, :].astype(F32) + back)
-
-    grad_q.second()
+    grad_p.second()
+    s_mix.forward()
+
+    s_enc.finish()
+    grad_k.gathered()
+    grad_k.product(enc, xenc)
+    s_eng.share(s_eng.total())
     grad_v.gathered()
     grad_v.product(enc, xenc)
-    s_mix.forward()
-    s_eng.share(s_eng.total())
-
-    gp[...] = grad_p.total()
-    grad_k.second()
     s_dng.forward()
     s_mix.forward_last()
+    grad_q.second()
+    gp[...] = grad_p.total()
+    s_eng.forward()
+    grad_k.second()
+    s_dng.forward_last()
     grad_v.second()
     gq[...] = grad_q.total().T
-    s_eng.forward()
-    s_dng.forward_last()
+    s_eng.forward_last()
     gk[...] = grad_k.total().T
     gv[...] = grad_v.total().T
-    s_eng.forward_last()
     for summed in (s_mix, s_dng, s_eng):
         summed.finish()
     for user in (*spreads, s_mix, s_dng, s_eng, grad_q, grad_k, grad_v, grad_p):
@@ -598,14 +590,38 @@
             copy.wait_send()
 
 
+def store_kernel(*refs):
+    count = len(refs) // 2
+    sems = refs[-1]
+    copies = [pltpu.make_async_copy(refs[i], refs[count + i], sems.at[i]) for i in range(count)]
+    for copy in copies:
+        copy.start()
+    for copy in copies:
+        copy.wait()
+
+
+def store(results):
+    anywhere = pl.BlockSpec(memory_space=pl.ANY)
+    return pl.pallas_call(
+        store_kernel,
+        out_shape=tuple(jax.ShapeDtypeStruct(array.shape, array.dtype) for array in results),
+        in_specs=[pl.BlockSpec(memory_space=pltpu.VMEM)] * len(results),
+        out_specs=[anywhere] * len(results),
+        scratch_shapes=[pltpu.SemaphoreType.DMA((len(results),))],
+        compiler_params=pltpu.CompilerParams(vmem_limit_bytes=1024 * 1024),
+        name="store",
+    )(*(pltpu.with_memory_space_constraint(array, pltpu.VMEM) for array in results))
+
+
 def body(enc, dec, grad_out, w_query, w_key, w_value, w_out, enc_len, dec_len, device_perm, slot_offset):
     anywhere = pl.BlockSpec(memory_space=pl.ANY)
-    scalars = pl.BlockSpec(memory_space=pltpu.SMEM)
     vmem = pltpu.VMEM
     dma = pltpu.SemaphoreType.DMA
     scratch = [
         vmem((ENC, D), BF16), vmem((DEC, D), BF16), vmem((DEC, D), BF16),
         vmem((D, COLS), BF16), vmem((D, COLS), BF16), vmem((D, COLS), BF16), vmem((COLS, D), BF16),
+        pltpu.SMEM((SLOTS, SLOTS), jnp.int32), pltpu.SMEM((SLOTS, SLOTS), jnp.int32),
+        pltpu.SMEM((SLOTS,), jnp.int32), pltpu.SMEM((SLOTS,), jnp.int32),
         vmem((3, DEC, 1024), BF16), vmem((3, DEC, 1024), BF16), vmem((3, ENC, 1024), BF16),
         vmem((256, ENC), BF16), vmem((ENC, 256), BF16), vmem((DEC, 256), F32),
         vmem((DEC, COLS), F32), vmem((ENC, COLS), F32),
@@ -626,17 +642,17 @@
     scratch += [vmem((4, COLS, 256), BF16)] * 4
     scratch += [vmem((3, COLS, 256), BF16)] * 4
     scratch += [
-        dma((7,)), dma((16,)), dma((16,)), dma((16,)), dma((16,)), dma((16,)), dma((16,)),
-        dma((3, 19)), dma((3, 19)), dma((3, 11)), dma((3, 11)),
+        dma((11,)), dma((16,)), dma((16,)), dma((16,)), dma((16,)), dma((16,)), dma((16,)),
+        dma((3, 19)), dma((3, 19)), dma((3, 15)), dma((3, 15)),
         dma((4, 6)), dma((4, 6)),
     ]
-    return pl.pallas_call(
+    results = pl.pallas_call(
         kernel,
         out_shape=(
             vmem((DEC, D), BF16), vmem((DEC, D), BF16), vmem((ENC, D), BF16),
             vmem((256, COLS), F32), vmem((256, COLS), F32), vmem((256, COLS), F32), vmem((COLS, 256), F32),
         ),
-        in_specs=[anywhere] * 7 + [scalars] * 4,
+        in_specs=[anywhere] * 11,
         out_specs=[pl.BlockSpec(memory_space=vmem)] * 7,
         scratch_shapes=scratch,
         compiler_params=pltpu.CompilerParams(
@@ -644,6 +660,7 @@
         ),
         name="cross_attention",
     )(enc, dec, grad_out, w_query, w_key, w_value, w_out, enc_len, dec_len, device_perm, slot_offset)
+    return store(results)
 
 
 def solution(mesh):

time: 91.1 us -> 86.1 us (0.945); the launches traced: 89.6 us -> 86 us
  local copies, waits for them, and re-layouts: 6.78 us -> 0 us
  Pallas kernels: 82.2 us -> 85.2 us
    unnamed x7 -> x0, local copies, waits for them, and re-layouts: 6.78 us -> none
    pallas_call x0 -> x1, Pallas kernels: none -> 3.03 us  [store(): pl.pallas_call(store_kernel, out_shape=tuple((jax.ShapeDtypeStruct(array....]
where the time goes in v4:
time: 86.1 us; the launch traced here: 86 us
  Pallas kernels  85.2 us (99%)
    pallas_call x1, Pallas kernels, body(): pl.pallas_call(kernel, out_shape=(vmem((DEC, D), BF16), vmem((DEC, D), BF...  82.1 us
    pallas_call x1, Pallas kernels, store(): pl.pallas_call(store_kernel, out_shape=tuple((jax.ShapeDtypeStruct(array....  3.03 us

profile of v4, /device:TPU:0, one launch (start us, length us, event | category | flops | bytes accessed | tf_op | source)
XLA Modules:
  0.0 86.0 jit_solution(12784801632011627353)
XLA Ops:
  0.6 82.1 %cross_attention.1 = (bf16[256,4096]{1,0:T(8,128)(2,1)S(1)}, bf16[256,4096]{1,0:T(8,128)(2,1)S(1)}, bf16[128,4096]{1,0:T(8,128)(2,1)S(1)}, f32[256,512]{1,0:T(8,...) custom-call(bf16[128,4096]{1,0:T(8,128)(2,1)} %enc_h.1, ...), custom_call_target="tpu_custom_call" | custom-call | tf_op jit(solution)/shard_map/cross_attention/pallas_call | solution.py:649
  82.8 3.0 %store.1 = (bf16[256,4096]{1,0:T(8,128)(2,1)}, bf16[256,4096]{1,0:T(8,128)(2,1)}, bf16[128,4096]{1,0:T(8,128)(2,1)}, f32[256,512]{1,0:T(8,128)}, f32[256,512]{1,...) custom-call(bf16[256,4096]{1,0:T(8,128)(2,1)S(1)} %get-tuple-element.14.refs_0_, ...), custom_call_target="tpu_custom_call" | custom-call | tf_op jit(solution)/shard_map/store/pallas_call | solution.py:605

commit v5 on v4

--- a/solution.py
+++ b/solution.py
@@ -487,12 +487,6 @@
         raw_d[:, head(h)] = heads_out
         att[:, head(h)] = heads_out.astype(BF16)
         fp[at.x, head(h), :] = heads_out.T.astype(BF16)
-    grad_p.gather()
-
-    for piece in range(4):
-        cols = quarter(piece)
-        p_mix[:, cols] = dot_nn(att[...], wo[:, cols]).astype(BF16)
-        s_mix.over_core(piece)
 
     for h in range(2):
         keys, values = k_in[:, head(h)], v_in[:, head(h)]
@@ -507,7 +501,13 @@
         dqb[:, head(h)] = dq_raw.astype(BF16)
         fq[at.z, head(h), :] = (dq_raw * r_dec[:, :1]).T.astype(BF16)
     exchange(g_out, g_in, g_send, g_recv)
+    grad_p.gather()
     grad_q.gather()
+    for piece in range(4):
+        cols = quarter(piece)
+        p_mix[:, cols] = dot_nn(att[...], wo[:, cols]).astype(BF16)
+        s_mix.over_core(piece)
+
     s_mix.first()
 
     for piece in range(4):
@@ -515,11 +515,11 @@
         p_dec[:, cols] = dot_nt(dqb[...], wq[cols, :]).astype(BF16)
         s_dng.over_core(piece)
 
-    grad_p.gather_again()
     s_dng.first()
     s_go.over_core()
     s_dec.over_core()
     s_mix.second()
+    grad_p.gather_again()
     grad_q.gather_again()
 
     exchanged(g_out, g_in, g_send, g_recv)
@@ -540,45 +540,41 @@
         p_enc[:, cols] = (dot_nt(dkb[...], wk[cols, :]) + dot_nt(dvb[...], wv[cols, :])).astype(BF16)
         s_eng.over_core(piece)
 
+    mine_d = rows_of((at.c * 4 + at.y) * 32, 32)
     s_dng.second()
-
     s_go.finish()
     grad_p.gathered()
     grad_p.product(go, xgo)
     s_eng.first()
-    mine_d = rows_of((at.c * 4 + at.y) * 32, 32)
-    s_mix.share(dec[mine_d, :].astype(F32) + s_mix.total())
-
-    s_enc.over_core()
     grad_k.gather_again()
     grad_v.gather_again()
     s_dec.finish()
     grad_q.gathered()
     grad_q.product(dec, xdec)
+    s_mix.share(dec[mine_d, :].astype(F32) + s_mix.total())
+    s_enc.over_core()
     s_eng.second()
-
     total = s_dng.total()
     unit = dec[mine_d, :].astype(F32) * r_dec[mine_d, :1]
     mean = jnp.mean(total * unit, axis=1, keepdims=True)
     back = r_dec[mine_d, :1] * (total - unit * mean)
     s_dng.share(go[mine_d, :].astype(F32) + back)
     grad_p.second()
-    s_mix.forward()
-
     s_enc.finish()
     grad_k.gathered()
     grad_k.product(enc, xenc)
-    s_eng.share(s_eng.total())
     grad_v.gathered()
     grad_v.product(enc, xenc)
+    s_mix.forward()
+    s_eng.share(s_eng.total())
     s_dng.forward()
+    grad_q.second()
     s_mix.forward_last()
-    grad_q.second()
+    grad_k.second()
+    grad_v.second()
     gp[...] = grad_p.total()
     s_eng.forward()
-    grad_k.second()
     s_dng.forward_last()
-    grad_v.second()
     gq[...] = grad_q.total().T
     s_eng.forward_last()
     gk[...] = grad_k.total().T

time: 86.1 us -> 84.4 us (0.980)
  Pallas kernels: 85.2 us -> 83.5 us
    pallas_call x1, Pallas kernels: 82.1 us -> 80.5 us  [body(): pl.pallas_call(kernel, out_shape=(vmem((DEC, D), BF16), vmem((DEC, D), BF...]
where the time goes in v5:
time: 84.4 us; the launch traced here: 84.3 us
  Pallas kernels  83.5 us (99%)
    pallas_call x1, Pallas kernels, body(): pl.pallas_call(kernel, out_shape=(vmem((DEC, D), BF16), vmem((DEC, D), BF...  80.5 us
    pallas_call x1, Pallas kernels, store(): pl.pallas_call(store_kernel, out_shape=tuple((jax.ShapeDtypeStruct(array....  3.03 us

profile of v5, /device:TPU:0, one launch (start us, length us, event | category | flops | bytes accessed | tf_op | source)
XLA Modules:
  0.0 84.3 jit_solution(6451270153902026523)
XLA Ops:
  0.6 80.5 %cross_attention.1 = (bf16[256,4096]{1,0:T(8,128)(2,1)S(1)}, bf16[256,4096]{1,0:T(8,128)(2,1)S(1)}, bf16[128,4096]{1,0:T(8,128)(2,1)S(1)}, f32[256,512]{1,0:T(8,...) custom-call(bf16[128,4096]{1,0:T(8,128)(2,1)} %enc_h.1, ...), custom_call_target="tpu_custom_call" | custom-call | tf_op jit(solution)/shard_map/cross_attention/pallas_call | solution.py:645
  81.1 3.0 %store.1 = (bf16[256,4096]{1,0:T(8,128)(2,1)}, bf16[256,4096]{1,0:T(8,128)(2,1)}, bf16[128,4096]{1,0:T(8,128)(2,1)}, f32[256,512]{1,0:T(8,128)}, f32[256,512]{1,...) custom-call(bf16[256,4096]{1,0:T(8,128)(2,1)S(1)} %get-tuple-element.14.refs_0_, ...), custom_call_target="tpu_custom_call" | custom-call | tf_op jit(solution)/shard_map/store/pallas_call | solution.py:601

commit v6 on v5

--- a/solution.py
+++ b/solution.py
@@ -339,7 +339,7 @@
     mixed, decg, encg, gq, gk, gv, gp,
     enc, dec, go, wq, wk, wv, wo,
     enc_len, dec_len, perm, offset,
-    xdec, xgo, xenc,
+    xdec, xgo, xenc, zenc,
     pack_ref, unpack_ref, mask_ref,
     raw_d, raw_e, qu, qa, ku, kb, r_dec, qb, up, k_out, v_out, k_in, v_in, g_out, g_in, probs, att, dqb, dkb, dvb,
     p_mix, c_mix, y_mix, p_dec, c_dec, y_dec, p_enc, c_enc, y_enc,
@@ -378,7 +378,8 @@
     s_dec = Spread(at, at.along_z, 2, dec_h, xdec, x_send.at[0], x_recv.at[0])
     s_go = Spread(at, at.along_x, 2, go_h, xgo, x_send.at[1], x_recv.at[1])
     s_enc = Spread(at, at.along_x, 1, enc_h, xenc, x_send.at[2], x_recv.at[2])
-    spreads = (s_go, s_dec, s_enc)
+    s_enz = Spread(at, at.along_z, 1, enc_h, zenc, x_send.at[3], x_recv.at[3])
+    spreads = (s_go, s_dec, s_enc, s_enz)
     s_go.over_line()
     s_dec.over_line()
 
@@ -468,7 +469,7 @@
 
     grad_q = weight(0, at.along_z, at.along_x, fq, pq, zq)
     grad_k = weight(1, at.along_x, at.along_z, fk, pk, zk)
-    grad_v = weight(2, at.along_x, at.along_z, fv, pv, zv)
+    grad_v = weight(2, at.along_z, at.along_x, fv, pv, zv)
     grad_p = weight(3, at.along_x, at.along_z, fp, pp, zp)
     s_mix = Summed(at, p_mix, c_mix, y_mix, mixed, s_send.at[0], s_recv.at[0])
     s_dng = Summed(at, p_dec, c_dec, y_dec, decg, s_send.at[1], s_recv.at[1])
@@ -530,10 +531,11 @@
         fk[at.x, head(h), :] = dk_raw.T.astype(BF16)
         dvalue = dot_nn(unpack_ref[...], g_in[:, head(h + 2)])
         dvb[:, head(h)] = dvalue.astype(BF16)
-        fv[at.x, head(h), :] = dvalue.T.astype(BF16)
+        fv[at.z, head(h), :] = dvalue.T.astype(BF16)
     grad_k.gather()
     grad_v.gather()
     s_enc.over_line()
+    s_enz.over_line()
 
     for piece in range(4):
         cols = quarter(piece)
@@ -553,6 +555,7 @@
     grad_q.product(dec, xdec)
     s_mix.share(dec[mine_d, :].astype(F32) + s_mix.total())
     s_enc.over_core()
+    s_enz.over_core()
     s_eng.second()
     total = s_dng.total()
     unit = dec[mine_d, :].astype(F32) * r_dec[mine_d, :1]
@@ -563,8 +566,9 @@
     s_enc.finish()
     grad_k.gathered()
     grad_k.product(enc, xenc)
+    s_enz.finish()
     grad_v.gathered()
-    grad_v.product(enc, xenc)
+    grad_v.product(enc, zenc)
     s_mix.forward()
     s_eng.share(s_eng.total())
     s_dng.forward()
@@ -618,7 +622,7 @@
         vmem((D, COLS), BF16), vmem((D, COLS), BF16), vmem((D, COLS), BF16), vmem((COLS, D), BF16),
         pltpu.SMEM((SLOTS, SLOTS), jnp.int32), pltpu.SMEM((SLOTS, SLOTS), jnp.int32),
         pltpu.SMEM((SLOTS,), jnp.int32), pltpu.SMEM((SLOTS,), jnp.int32),
-        vmem((3, DEC, 1024), BF16), vmem((3, DEC, 1024), BF16), vmem((3, ENC, 1024), BF16),
+        vmem((3, DEC, 1024), BF16), vmem((3, DEC, 1024), BF16), vmem((3, ENC, 1024), BF16), vmem((3, ENC, 1024), BF16),
         vmem((256, ENC), BF16), vmem((ENC, 256), BF16), vmem((DEC, 256), F32),
         vmem((DEC, COLS), F32), vmem((ENC, COLS), F32),
         vmem((DEC, COLS), F32), vmem((2, DEC, 128), F32),
@@ -639,7 +643,7 @@
     scratch += [vmem((3, COLS, 256), BF16)] * 4
     scratch += [
         dma((11,)), dma((16,)), dma((16,)), dma((16,)), dma((16,)), dma((16,)), dma((16,)),
-        dma((3, 19)), dma((3, 19)), dma((3, 15)), dma((3, 15)),
+        dma((4, 19)), dma((4, 19)), dma((3, 15)), dma((3, 15)),
         dma((4, 6)), dma((4, 6)),
     ]
     results = pl.pallas_call(

time: 84.4 us -> 82 us (0.972)
  Pallas kernels: 83.5 us -> 80.9 us
    pallas_call x1, Pallas kernels: 80.5 us -> 77.9 us  [body(): pl.pallas_call(kernel, out_shape=(vmem((DEC, D), BF16), vmem((DEC, D), BF...]
where the time goes in v6:
time: 82 us; the launch traced here: 81.7 us
  Pallas kernels  80.9 us (99%)
    pallas_call x1, Pallas kernels, body(): pl.pallas_call(kernel, out_shape=(vmem((DEC, D), BF16), vmem((DEC, D), BF...  77.9 us
    pallas_call x1, Pallas kernels, store(): pl.pallas_call(store_kernel, out_shape=tuple((jax.ShapeDtypeStruct(array....  3.03 us

profile of v6, /device:TPU:0, one launch (start us, length us, event | category | flops | bytes accessed | tf_op | source)
XLA Modules:
  0.0 81.7 jit_solution(3395000394905251946)
XLA Ops:
  0.6 77.9 %cross_attention.1 = (bf16[256,4096]{1,0:T(8,128)(2,1)S(1)}, bf16[256,4096]{1,0:T(8,128)(2,1)S(1)}, bf16[128,4096]{1,0:T(8,128)(2,1)S(1)}, f32[256,512]{1,0:T(8,...) custom-call(bf16[128,4096]{1,0:T(8,128)(2,1)} %enc_h.1, ...), custom_call_target="tpu_custom_call" | custom-call | tf_op jit(solution)/shard_map/cross_attention/pallas_call | solution.py:649
  78.5 3.0 %store.1 = (bf16[256,4096]{1,0:T(8,128)(2,1)}, bf16[256,4096]{1,0:T(8,128)(2,1)}, bf16[128,4096]{1,0:T(8,128)(2,1)}, f32[256,512]{1,0:T(8,128)}, f32[256,512]{1,...) custom-call(bf16[256,4096]{1,0:T(8,128)(2,1)S(1)} %get-tuple-element.14.refs_0_, ...), custom_call_target="tpu_custom_call" | custom-call | tf_op jit(solution)/shard_map/store/pallas_call | solution.py:605
